TPU v7x, 32 devices: a whole 2x2x4 slice. The times are simulated.
32 devices in a mesh: grp: 2 (over y), tm: 4 (over z), spin: 2 (over core), rows: 2 (over x).
Axes of the slice: x: 2, y: 2, z: 4, core: 2. Of those that a mesh axis runs over, the one named last changes fastest.
Arguments:
- ising_field: int32 [32, 768], P(('grp', 'tm')), parts along dimension 0, may hold values from 0 to 1
- bond_sites: int32 [3072, 2], replicated, may hold values from 0 to 767
- hopping: float32 [3072], replicated, may hold values from 0.5 to 2
- tile_cols: int32 [6, 3], replicated, may hold values from 0 to 5, as said below
Outputs:
- xcorr: float32 [2, 8, 768, 768], P('spin', ('grp', 'tm'), None, 'rows'), parts along dimension 1
There are 2 independent parts, one for each index of `grp`. A program takes and returns all parts, laid end to end along the dimension named above; an argument that names none is the same for every part. Nothing has to cross between parts.
Inputs may be any that keep to these rules, and one draw needn't show every extreme that they name: `ising_field`: 0 stands for the field value -1 and 1 for +1. `bond_sites`: A bond whose tile pair is not in tile_cols adds nothing to H, because tile_mask removes it; its entry in `hopping` is not zero. `tile_cols`: row r lists r first and then the two tiles beside r on a cycle through all 6 tiles drawn from the seed, so each tile row names 3 distinct tiles and the pattern is symmetric.
All inputs are finite; a program needn't handle non-finite values.
Results may differ from a plain program's by a relative error of at most 0.0003.
Values sent between devices are 32-bit elements; how exact they have to be, the bound alone decides.
A program may use at most 64 MiB of HBM per device.

v0:
```python
import math

import jax
import jax.numpy as jnp
from jax import lax
from jax.sharding import PartitionSpec as P

series_terms = 4


def from_behind(x, axis, by):
    size = lax.axis_size(axis)
    return lax.ppermute(x, axis, [(i, (i + by) % size) for i in range(size)])


def partner_2(value, axis, bit):
    mask = 2**bit
    pairs = [(source, source ^ mask) for source in range(lax.axis_size(axis))]
    return lax.ppermute(value, axis, pairs)


def matmul_hi(left, right):
    return jnp.dot(left, right, precision=lax.Precision.HIGHEST, preferred_element_type=jnp.float32)


def build_kinetic(bond_sites, hopping, tile_cols, matrix_order, hop_scale):
    n_tiles = tile_cols.shape[0]
    tile_len = matrix_order // n_tiles
    tile_mask = jnp.any(
        tile_cols[:, :, None] == jnp.arange(n_tiles, dtype=jnp.int32)[None, None, :], axis=1
    ).astype(jnp.float32)
    site_from = bond_sites[:, 0]
    site_to = bond_sites[:, 1]
    kept_mask = tile_mask[site_from // tile_len, site_to // tile_len]
    weights = hopping * kept_mask
    hop_matrix = jnp.zeros((matrix_order, matrix_order), jnp.float32)
    hop_matrix = hop_matrix.at[site_from, site_to].add(weights).at[site_to, site_from].add(weights)
    return jnp.eye(matrix_order, dtype=jnp.float32) + hop_scale * hop_matrix


def fold_product(current, piece):
    return matmul_hi(piece, current)


def fold_series(power, green, square_it, apply_it):

    def accumulate(totals, piece, start):
        power_total, green_total = totals
        if square_it:
            power_total = matmul_hi(piece, power)
        if apply_it:
            green_total = matmul_hi(piece, green)
        return (power_total, green_total)

    return accumulate


def per_device(ising_field, bond_sites, hopping, tile_cols):
    slices_here, matrix_order = ising_field.shape
    n_tiles, tile_count = tile_cols.shape
    tile_len = matrix_order // n_tiles
    col_width = matrix_order // lax.axis_size("rows")
    n_time = lax.axis_size("tm")
    total_slices = slices_here * n_time
    coupling = 1.5 / math.sqrt(total_slices)
    kinetic = build_kinetic(bond_sites, hopping, tile_cols, matrix_order, 0.5 / total_slices)
    spin_sign = 1.0 - 2.0 * lax.axis_index("spin").astype(jnp.float32)
    spins_pm = (2 * ising_field - 1).astype(jnp.float32)
    factors = jnp.exp(spin_sign * coupling * spins_pm)
    offset = lax.axis_index("rows") * col_width
    tiled = kinetic.reshape(n_tiles, tile_len, n_tiles, tile_len).transpose(0, 2, 1, 3)
    k_tiles = tiled[jnp.arange(n_tiles, dtype=jnp.int32)[:, None], tile_cols]
    cluster = factors[0][:, None] * lax.dynamic_slice_in_dim(kinetic, offset, col_width, 1)

    def slice_step(slice_pos, current):
        gathered = current.reshape(n_tiles, tile_len, col_width)[tile_cols]
        product = jnp.einsum(
            "rjab,rjbc->rac",
            k_tiles,
            gathered,
            precision=lax.Precision.HIGHEST,
            preferred_element_type=jnp.float32,
        )
        return factors[slice_pos][:, None] * product.reshape(matrix_order, col_width)

    cluster = lax.fori_loop(1, slices_here, slice_step, cluster)
    time_steps = n_time.bit_length() - 1
    propagator = cluster
    for level in range(time_steps):
        distant = from_behind(propagator, "tm", -(1 << level))
        empty = jnp.zeros((matrix_order, col_width), jnp.float32)
        propagator = fold_product(propagator, lax.all_gather(distant, "rows", axis=1, tiled=True))
    col_max = lax.pmax(jnp.max(jnp.sum(propagator, axis=0)), "rows")
    power = propagator / (2.0 * col_max)
    row_ids = jnp.arange(matrix_order, dtype=jnp.int32)[:, None]
    col_ids = offset + jnp.arange(col_width, dtype=jnp.int32)[None, :]
    eye_cols = (row_ids == col_ids).astype(jnp.float32)
    green = eye_cols - power
    for level in range(series_terms):
        square_it = level + 1 < series_terms
        apply_it = level > 0
        empty = jnp.zeros((matrix_order, col_width), jnp.float32)
        folder = fold_series(power, green, square_it, apply_it)
        next_power, green_term = folder(
            (empty, empty), lax.all_gather(power, "rows", axis=1, tiled=True), jnp.int32(0)
        )
        if apply_it:
            green = green + green_term
        if square_it:
            power = next_power
    partner = partner_2(green, "spin", 0)
    rows_block = lax.all_to_all(partner, "rows", split_axis=0, concat_axis=1, tiled=True)
    other_trans = rows_block.T
    xcorr = green * (eye_cols - other_trans)
    return xcorr[None, None]


def solution(mesh):
    placed = (P(("grp", "tm"), None), P(), P(), P())
    return jax.shard_map(
        per_device,
        mesh=mesh,
        in_specs=placed,
        out_specs=P("spin", ("grp", "tm"), None, "rows"),
        check_vma=False,
    )
```

profile of v0, /device:TPU:0, one launch (start us, length us, event | category | flops | bytes accessed | tf_op | source)
XLA Modules:
  0.0 485.7 jit_solution(5524657605917395206)
XLA Ops:
  6.5 0.8 fusion.10
  7.3 0.7 fusion.14
  8.0 1.0 fusion.7
  9.0 0.1 and_reduce_fusion
  9.1 0.8 multiply_reduce_fusion
  9.9 13.4 %gather_fusion.1 = f32[3072]{0:T(1024)S(1)} fusion(f32[6,6]{1,0:T(8,128)S(1)} %convert_element_type.19, s32[3072]{0:T(1024)S(1)} %bitcast.64), kind=kCustom, calls=%fused_computation.1 | custom fusion | bytes 49152 | tf_op jit(solution)/shard_map/gather | solution.py:34
  23.4 17.1 %scatter_custom_fusion = f32[589824]{0:T(1024)S(1)} fusion(s32[3072]{0:T(1024)S(1)} %get-tuple-element.158, f32[3072]{0:T(1024)S(1)} %mul.88, f32[]{:T(128)} %constant.99.clone.1), kind=kCustom, calls=%fused_computation.20 | custom fusion | flops 3072 | bytes 2359300
  40.6 17.8 %scatter_fusion = f32[589824]{0:T(1024)S(1)} fusion(f32[589824]{0:T(1024)S(1)} %scatter_custom_fusion, s32[3072]{0:T(1024)S(1)} %get-tuple-element.157, f32[3072]{0:T(1024)S(1)} %mul.88), kind=kCustom, calls=%fused_computation.4 | custom fusion | flops 3072 | bytes 49152
  58.4 1.6 broadcast_multiply_fusion
  59.9 3.4 reshape.67
  63.3 1.8 convert_add_fusion
  65.2 0.6 copy-done.8
  65.8 1.9 reshape.56
  67.6 3.7 copy.20
  71.6 0.2 dynamic-slice_multiply_fusion
  71.7 3.4 gather_fusion.2
  75.1 31.4 %while.15 = (s32[]{:T(128)}, f32[768,384]{1,0:T(8,128)S(1)}, f32[4,768]{1,0:T(4,128)}, s32[6,3]{0,1:T(4,128)S(1)}, f32[6,3,128,128]{3,2,1,0:T(8,128)}, /*index=5*/s32[]{:T(128)}, s32[]{:T(128)}, s32[]{:T(128)}) while((s32[]{:T(128)}, f32[768,384]{1,0:T(8,128)S(1)}, f32[4,768]{1,0:T(4,128)}, s32[6,3]{0,1:T(4,128)S(1)}, ...), condition=%wide.region_4.5_spmd, body=%wide.region_3.4_spmd.sunk | while | flops 1359250432 | bytes 20068060 | solution.py:86
  75.1 0.1 copy.22
  75.3 0.8 copy-done
  76.2 2.0 gather_fusion
  78.2 5.2 %fusion.43 = f32[6,384,128,1]{1,2,3,0:T(8,128)} fusion(f32[6,3,128,384]{3,2,1,0:T(8,128)S(1)} %bitcast.62, f32[6,3,128,128]{3,2,1,0:T(8,128)} %get-tuple-element.210), kind=kOutput, calls=%fused_computation.62.clone.1 | convolution fusion | flops 1358954496 | bytes 5898240 | tf_op jit(solution)/shard_map/while/body/eval_jaxpr/rjab,rjbc->rac/dot_general | solution.py:77
  83.4 0.7 dynamic-slice_reduce_fusion.2
  84.2 1.4 bitcast_multiply_fusion.2
  85.6 0.1 copy.22
  85.8 0.8 copy-done
  86.6 2.0 gather_fusion
  88.7 5.2 %fusion.43 = f32[6,384,128,1]{1,2,3,0:T(8,128)} fusion(f32[6,3,128,384]{3,2,1,0:T(8,128)S(1)} %bitcast.62, f32[6,3,128,128]{3,2,1,0:T(8,128)} %get-tuple-element.210), kind=kOutput, calls=%fused_computation.62.clone.1 | convolution fusion | flops 1358954496 | bytes 5898240 | tf_op jit(solution)/shard_map/while/body/eval_jaxpr/rjab,rjbc->rac/dot_general | solution.py:77
  93.9 0.7 dynamic-slice_reduce_fusion.2
  94.6 1.4 bitcast_multiply_fusion.2
  96.1 0.1 copy.22
  96.3 0.8 copy-done
  97.1 2.0 gather_fusion
  99.2 5.2 %fusion.43 = f32[6,384,128,1]{1,2,3,0:T(8,128)} fusion(f32[6,3,128,384]{3,2,1,0:T(8,128)S(1)} %bitcast.62, f32[6,3,128,128]{3,2,1,0:T(8,128)} %get-tuple-element.210), kind=kOutput, calls=%fused_computation.62.clone.1 | convolution fusion | flops 1358954496 | bytes 5898240 | tf_op jit(solution)/shard_map/while/body/eval_jaxpr/rjab,rjbc->rac/dot_general | solution.py:77
  104.4 0.7 dynamic-slice_reduce_fusion.2
  105.1 1.4 bitcast_multiply_fusion.2
  106.6 5.1 %collective-permute-start = (f32[768,384]{1,0:T(8,128)S(1)}, f32[768,384]{1,0:T(8,128)S(1)}, u32[]{:S(2)}, u32[]{:S(2)}) collective-permute-start(f32[768,384]{1,0:T(8,128)S(1)} %get-tuple-element.137), channel_id=1, source_target_pairs={{0,12},{4,0},{8,4},{12,8},{1,13},{5,1},{9,5},{13,9},{2,14},{6,2},{... | collective-permute-start | bytes 3538952 | tf_op jit(solution)/shard_map/ppermute | solution.py:13
  111.7 25.2 %collective-permute-done = f32[768,384]{1,0:T(8,128)S(1)} collective-permute-done((f32[768,384]{1,0:T(8,128)S(1)}, f32[768,384]{1,0:T(8,128)S(1)}, u32[]{:S(2)}, u32[]{:S(2)}) %collective-permute-start) | collective-permute-done | bytes 1179680 | tf_op jit(solution)/shard_map/ppermute | solution.py:13
  136.9 1.0 copy-done.5
  137.9 0.2 all-gather.9.cloned.1.call-start
  138.2 37.9 %all-gather.7.cloned.1.call-done = f32[768,768]{1,0:T(8,128)} async-done(((f32[768,384]{1,0:T(8,128)}), f32[768,768]{1,0:T(8,128)}) %all-gather.7.cloned.1.call-update) | async-done | bytes 2359312 | tf_op jit(solution)/shard_map/all_gather | solution.py:92
  176.1 5.5 %fusion.17 = f32[768,384]{1,0:T(8,128)S(1)} fusion(f32[768,768]{1,0:T(8,128)} %all-gather.7.cloned.1.call-done, f32[768,384]{1,0:T(8,128)S(1)} %get-tuple-element.137), kind=kOutput, calls=%fused_computation.63 | convolution fusion | flops 2717908992 | bytes 4718592 | tf_op jit(solution)/shard_map/dot_general | solution.py:23
  181.6 2.5 collective-permute-start.1
  184.0 51.5 %collective-permute-done.1 = f32[768,384]{1,0:T(8,128)S(1)} collective-permute-done((f32[768,384]{1,0:T(8,128)S(1)}, f32[768,384]{1,0:T(8,128)S(1)}, u32[]{:S(2)}, u32[]{:S(2)}) %collective-permute-start.1) | collective-permute-done | bytes 1179680 | tf_op jit(solution)/shard_map/ppermute | solution.py:13
  235.5 1.0 copy-done.6
  236.6 36.2 %all-gather.9.cloned.1.call-done = f32[768,768]{1,0:T(8,128)} async-done(((f32[768,384]{1,0:T(8,128)}), f32[768,768]{1,0:T(8,128)}) %all-gather.9.cloned.1.call-update) | async-done | bytes 2359312 | tf_op jit(solution)/shard_map/all_gather | solution.py:92
  272.8 5.5 %fusion.15 = (f32[384]{0:T(512)S(1)}, f32[768,384]{1,0:T(8,128)S(1)}) fusion(f32[768,768]{1,0:T(8,128)} %all-gather.9.cloned.1.call-done, f32[768,384]{1,0:T(8,128)S(1)} %fusion.17), kind=kOutput, calls=%fused_computation.61 | convolution fusion | flops 2718203392 | bytes 4720128 | tf_op jit(solution)/shard_map/dot_general | solution.py:23
  278.3 0.6 reduce_max.9
  278.9 5.5 %pmax.7 = f32[]{:T(128)} all-reduce(f32[]{:T(128)} %reduce_max.9), channel_id=1, replica_groups=mesh['grp'=2,'tm'=4,'spin'=2,'rows'=2] {'rows'}, use_global_device_ids=true, to_apply=%region_7.8 | all-reduce | flops 1 | bytes 8 | tf_op jit(solution)/shard_map/pmax | solution.py:93
  285.1 1.1 broadcast_divide_fusion
  286.3 36.2 %all-gather.11.cloned.1.call-done = f32[768,768]{1,0:T(8,128)} async-done(((f32[768,384]{1,0:T(8,128)}), f32[768,768]{1,0:T(8,128)}) %all-gather.11.cloned.1.call-update) | async-done | bytes 2359312 | tf_op jit(solution)/shard_map/all_gather | solution.py:105
  322.5 6.5 %fusion.18 = f32[768,384]{1,0:T(8,128)} fusion(f32[768,768]{1,0:T(8,128)} %all-gather.11.cloned.1.call-done, f32[768,384]{1,0:T(8,128)S(1)} %copy-done.1), kind=kOutput, calls=%fused_computation.64 | convolution fusion | flops 2717908992 | bytes 4718592 | tf_op jit(solution)/shard_map/dot_general | solution.py:23
  329.1 36.2 %all-gather.13.cloned.1.call-done = f32[768,768]{1,0:T(8,128)} async-done(((f32[768,384]{1,0:T(8,128)}), f32[768,768]{1,0:T(8,128)}) %all-gather.13.cloned.1.call-update) | async-done | bytes 2359312 | tf_op jit(solution)/shard_map/all_gather | solution.py:105
  365.2 6.5 %fusion.19 = f32[768,384]{1,0:T(8,128)} fusion(f32[768,768]{1,0:T(8,128)} %all-gather.13.cloned.1.call-done, f32[768,384]{1,0:T(8,128)S(1)} %copy-done.2), kind=kOutput, calls=%fused_computation.65 | convolution fusion | flops 2717908992 | bytes 4718592 | tf_op jit(solution)/shard_map/dot_general | solution.py:23
  371.8 0.3 all-gather.17.cloned.1.call-start
  372.0 36.0 %all-gather.15.cloned.1.call-done = f32[768,768]{1,0:T(8,128)} async-done(((f32[768,384]{1,0:T(8,128)}), f32[768,768]{1,0:T(8,128)}) %all-gather.15.cloned.1.call-update) | async-done | bytes 2359312 | tf_op jit(solution)/shard_map/all_gather | solution.py:105
  408.0 6.5 %fusion.20 = f32[768,384]{1,0:T(8,128)} fusion(f32[768,768]{1,0:T(8,128)} %all-gather.15.cloned.1.call-done, f32[768,384]{1,0:T(8,128)S(1)} %copy-done.3), kind=kOutput, calls=%fused_computation.66 | convolution fusion | flops 2717908992 | bytes 4718592 | tf_op jit(solution)/shard_map/dot_general | solution.py:23
  414.6 5.7 %convolution_add_fusion.2 = f32[768,384]{1,0:T(8,128)S(1)} fusion(f32[768,768]{1,0:T(8,128)} %all-gather.13.cloned.1.call-done, f32[768,384]{1,0:T(8,128)S(1)} %copy-done.1, s32[384]{0:T(512)S(1)} %iota_add_fusion), kind=kOutput, calls=%fused_computation.16 | convolution fusion | flops 2719088640 | bytes 4720128 | tf_op jit(solution)/shard_map/dot_general | solution.py:23
  420.3 3.9 convolution_add_fusion.1
  424.2 26.6 %all-gather.17.cloned.1.call-done = f32[768,768]{1,0:T(8,128)} async-done(((f32[768,384]{1,0:T(8,128)}), f32[768,768]{1,0:T(8,128)}) %all-gather.17.cloned.1.call-update) | async-done | bytes 2359312 | tf_op jit(solution)/shard_map/all_gather | solution.py:105
  450.8 5.5 %convolution_add_fusion = f32[768,384]{1,0:T(8,128)S(1)} fusion(f32[768,384]{1,0:T(8,128)S(1)} %convolution_add_fusion.1, f32[768,768]{1,0:T(8,128)} %all-gather.17.cloned.1.call-done), kind=kOutput, calls=%fused_computation.14 | convolution fusion | flops 2718203904 | bytes 4718592 | tf_op jit(solution)/shard_map/dot_general | solution.py:23
  456.4 2.8 collective-permute-done.2
  459.2 0.4 copy.17
  459.6 18.0 %all_to_all.19 = f32[2,384,384]{1,2,0:T(8,128)S(1)} all-to-all(f32[2,384,384]{1,2,0:T(8,128)S(1)} %copy.17), channel_id=1, replica_groups=mesh['grp'=2,'tm'=4,'spin'=2,'rows'=2] {'rows'}, dimensions={0} | all-to-all | bytes 2359296 | tf_op jit(solution)/shard_map/all_to_all | solution.py:112
  477.6 1.2 fusion.1
  (48 shorter events, 0.8 us)
Async XLA Ops:
  6.5 169.5 %all-gather.7.cloned.1.call-start = ((), (), s32[]{:S(2)}) async-start(), calls=%async_computation.1 | async-start | bytes 3538944 | tf_op jit(solution)/shard_map/all_gather | solution.py:92
  9.9 13.5 %copy-start.10 = (f32[3072]{0:T(1024)S(1)}, f32[3072]{0:T(1024)}, u32[]{:S(2)}) copy-start(f32[3072]{0:T(1024)} %param.8) | copy-start | bytes 36868
  63.3 1.9 copy-start.9
  65.2 0.6 copy-start.8
  71.7 3.4 copy-start.7
  75.1 1.0 copy-start
  85.6 1.0 copy-start
  96.1 1.0 copy-start
  106.6 30.3 %collective-permute-start = (f32[768,384]{1,0:T(8,128)S(1)}, f32[768,384]{1,0:T(8,128)S(1)}, u32[]{:S(2)}, u32[]{:S(2)}) collective-permute-start(f32[768,384]{1,0:T(8,128)S(1)} %get-tuple-element.137), channel_id=1, source_target_pairs={{0,12},{4,0},{8,4},{12,8},{1,13},{5,1},{9,5},{13,9},{2,14},{6,2},{... | collective-permute-start | bytes 3538952 | tf_op jit(solution)/shard_map/ppermute | solution.py:13
  136.9 1.0 copy-start.5
  137.9 134.9 %all-gather.9.cloned.1.call-start = ((), (), s32[]{:S(2)}) async-start(), calls=%async_computation.2 | async-start | bytes 3538944 | tf_op jit(solution)/shard_map/all_gather | solution.py:92
  181.6 54.0 %collective-permute-start.1 = (f32[768,384]{1,0:T(8,128)S(1)}, f32[768,384]{1,0:T(8,128)S(1)}, u32[]{:S(2)}, u32[]{:S(2)}) collective-permute-start(f32[768,384]{1,0:T(8,128)S(1)} %fusion.17), channel_id=1, source_target_pairs={{0,8},{4,12},{8,0},{12,4},{1,9},{5,13},{9,1},{13,5},{2,10},{6,14},... | collective-permute-start | bytes 3538952 | tf_op jit(solution)/shard_map/ppermute | solution.py:13
  235.5 1.0 copy-start.6
  236.6 85.9 %all-gather.11.cloned.1.call-start = ((), (), s32[]{:S(2)}) async-start(), calls=%async_computation.3 | async-start | bytes 3538944 | tf_op jit(solution)/shard_map/all_gather | solution.py:105
  286.2 36.3 %copy-start.1 = (f32[768,384]{1,0:T(8,128)S(1)}, f32[768,384]{1,0:T(8,128)}, u32[]{:S(2)}) copy-start(f32[768,384]{1,0:T(8,128)} %broadcast_divide_fusion) | copy-start | bytes 3538948
  286.2 79.0 %all-gather.13.cloned.1.call-start = ((), (), s32[]{:S(2)}) async-start(), calls=%async_computation.4 | async-start | bytes 3538944 | tf_op jit(solution)/shard_map/all_gather | solution.py:105
  329.0 36.3 %copy-start.2 = (f32[768,384]{1,0:T(8,128)S(1)}, f32[768,384]{1,0:T(8,128)}, u32[]{:S(2)}) copy-start(f32[768,384]{1,0:T(8,128)} %fusion.18) | copy-start | bytes 3538948
  329.0 79.0 %all-gather.15.cloned.1.call-start = ((), (), s32[]{:S(2)}) async-start(), calls=%async_computation.5 | async-start | bytes 3538944 | tf_op jit(solution)/shard_map/all_gather | solution.py:105
  371.8 36.3 %copy-start.3 = (f32[768,384]{1,0:T(8,128)S(1)}, f32[768,384]{1,0:T(8,128)}, u32[]{:S(2)}) copy-start(f32[768,384]{1,0:T(8,128)} %fusion.19) | copy-start | bytes 3538948
  371.8 79.0 %all-gather.17.cloned.1.call-start = ((), (), s32[]{:S(2)}) async-start(), calls=%async_computation.6 | async-start | bytes 3538944 | tf_op jit(solution)/shard_map/all_gather | solution.py:105
  414.6 5.7 %copy-start.4 = (f32[768,768]{1,0:T(8,128)S(1)}, f32[768,768]{1,0:T(8,128)}, u32[]{:S(2)}) copy-start(f32[768,768]{1,0:T(8,128)} %all-gather.15.cloned.1.call-done) | copy-start | bytes 7077892
  456.3 2.9 collective-permute-start.2
Sparse Core Ops, SparseCore 0:
  138.0 37.9 all-gather.6
  236.7 36.0 all-gather.8
  286.3 36.0 all-gather.10
  329.1 36.0 all-gather.12
  371.9 36.0 all-gather.14
  414.7 36.0 all-gather.16
where the time goes:
time: 487 us; the launch traced here: 486 us
  waiting for transfers between devices  289 us (59%)
  matrix products  61.3 us (13%)
  other arithmetic  49.2 us (10%)
  local copies, waits for them, and re-layouts  40.3 us (8%)
  blocking collectives  23.6 us (5%)
  between operations  14.3 us (3%)
  starting transfers between devices  8.25 us (2%)
    all_gather x4, waiting for transfers between devices, per_device(): lax.all_gather(power, 'rows', axis=1, tiled=True)  135 us
    ppermute x2, waiting for transfers between devices, from_behind(): return lax.ppermute(x, axis, [(i, (i + by) % size) for i in range(size)])  76.7 us
    all_gather x2, waiting for transfers between devices, per_device(): lax.all_gather(distant, 'rows', axis=1, tiled=True)  74.1 us
    dot_general x8, matrix products, matmul_hi(): jnp.dot(left, right, precision=lax.Precision.HIGHEST, preferred_element_t...  45.6 us
    unnamed x5, other arithmetic  35.9 us
    all_to_all x1, blocking collectives, per_device(): lax.all_to_all(partner, 'rows', split_axis=0, concat_axis=1, tiled=True)  18 us
    dot_general x3, matrix products, slice_step(): jnp.einsum('rjab,rjbc->rac', k_tiles, gathered, precision=lax.Precision.H...  15.6 us
    gather x1, local copies, waits for them, and re-layouts, build_kinetic(): kept_mask = tile_mask[site_from // tile_len, site_to // tile_len]  13.4 us
  transfers between devices with their start and end apart: 9, of which 9 were waited for; matrix products, arithmetic and copies ran while one was open for 2% of the time, Pallas kernels for 0%

commit v1 on v0

v1 whole, which is shorter than its diff:
```python
import functools
import math

import jax
import jax.numpy as jnp
from jax import lax
from jax.experimental import pallas as pl
from jax.experimental.pallas import tpu as pltpu
from jax.sharding import PartitionSpec as P

BF16 = jnp.bfloat16
F32 = jnp.float32
VMEM_BYTES = 48 * 1024 * 1024


def split(x):
    high = x.astype(BF16)
    return high, (x - high.astype(F32)).astype(BF16)


def dot(left, right):
    return jnp.dot(left, right, preferred_element_type=F32)


def cycle_order(tile_cols, n_tiles):
    order = [jnp.int32(0), tile_cols[0, 1]]
    for _ in range(n_tiles - 2):
        here = order[-1]
        order.append(tile_cols[here, 1] + tile_cols[here, 2] - order[-2])

    def place(tile):
        found = jnp.int32(0)
        for position, name in enumerate(order):
            found = jnp.where(name == tile, jnp.int32(position), found)
        return found

    return order, place


def kinetic_kernel(
    n_tiles, tile_len, hop_scale, chunk, tile_cols, sites, hopping, k_high, k_low, one_hot, w_high, w_low, total
):
    bonds = sites.shape[1]
    pairs = n_tiles // 2
    wide = 2 * tile_len
    order, _ = cycle_order(tile_cols, n_tiles)
    total[...] = jnp.zeros_like(total)
    row_ids = lax.broadcasted_iota(jnp.int32, (tile_len, chunk), 0)
    lane_ids = lax.broadcasted_iota(jnp.int32, (tile_len, tile_len), 1)

    def add_chunk(step, carry):
        begin = pl.multiple_of(step * chunk, chunk)
        site_from = sites[0:1, pl.ds(begin, chunk)]
        for p in range(n_tiles):
            hits = jnp.where(row_ids + order[p] * tile_len == site_from, 1.0, 0.0).astype(BF16)
            spots = [p + 1]
            if p == n_tiles - 1:
                spots.append(0)
            if p == 0:
                spots.append(n_tiles + 1)
            for spot in spots:
                one_hot[spot * tile_len : (spot + 1) * tile_len, :] = hits
        for part in range(chunk // tile_len):
            at = pl.multiple_of(begin + part * tile_len, tile_len)
            inside = slice(part * tile_len, (part + 1) * tile_len)
            site_to = jnp.broadcast_to(sites[1:2, pl.ds(at, tile_len)], (tile_len, tile_len)).T
            weight = jnp.broadcast_to(hopping[0:1, pl.ds(at, tile_len)], (tile_len, tile_len)).T
            high = weight.astype(BF16).astype(F32)
            low = weight - high
            for p in range(n_tiles):
                hit = lane_ids + order[p] * tile_len == site_to
                columns = slice(p * tile_len, (p + 1) * tile_len)
                w_high[inside, columns] = jnp.where(hit, high, 0.0).astype(BF16)
                w_low[inside, columns] = jnp.where(hit, low, 0.0).astype(BF16)
        for r in range(pairs):
            rows = slice(r * wide, (r + 2) * wide)
            columns = slice(r * wide, (r + 1) * wide)
            found = one_hot[rows, :]
            total[r] += dot(found, w_high[:, columns]) + dot(found, w_low[:, columns])
        return carry

    lax.fori_loop(0, bonds // chunk, add_chunk, 0)

    def tile_of(p, q):
        r, half = divmod(q, 2)
        row = (p - (2 * r - 1)) % n_tiles
        return r, slice(row * tile_len, (row + 1) * tile_len), slice(half * tile_len, (half + 1) * tile_len)

    diagonal = lax.broadcasted_iota(jnp.int32, (tile_len, tile_len), 0) == lane_ids
    k_high[...] = jnp.zeros_like(k_high)
    k_low[...] = jnp.zeros_like(k_low)
    for q in range(n_tiles):
        for p in ((q - 1) % n_tiles, q, (q + 1) % n_tiles):
            value = hop_scale * (total[tile_of(p, q)] + total[tile_of(q, p)].T)
            if p == q:
                value = jnp.where(diagonal, 1.0, 0.0) + value
            high, low = split(value)
            k_high[tile_of(p, q)] = high
            k_low[tile_of(p, q)] = low


def green_kernel(
    n_tiles, tile_len, slices_here, coupling, width,
    tile_cols, field, k_high, k_low, mine, sent,
    factors, y_high, y_low, x_full, x_high, x_low, b_high, b_low, u_full, t_full,
):
    total_slices = field.shape[0]
    order_len = n_tiles * tile_len
    pairs = n_tiles // 2
    wide = 2 * tile_len
    order, place = cycle_order(tile_cols, n_tiles)
    spin_sign = 1.0 - 2.0 * lax.axis_index("spin").astype(F32)
    start = lax.axis_index("tm") * slices_here
    strength = spin_sign * coupling
    for p in range(n_tiles):
        spins_pm = (2 * field[:, pl.ds(pl.multiple_of(order[p] * tile_len, tile_len), tile_len)] - 1).astype(F32)
        factors[:, p * tile_len : (p + 1) * tile_len] = jnp.exp(strength * spins_pm)

    def keep(slot, r, value):
        parts = split(value)
        for ref, part in zip((y_high, y_low), parts):
            ref[slot, :, tile_len + r * wide : tile_len + (r + 1) * wide] = part
            if r == 0:
                ref[slot, :, tile_len + order_len : 2 * tile_len + order_len] = part[:, :tile_len]
            if r == pairs - 1:
                ref[slot, :, :tile_len] = part[:, tile_len:]

    first = factors[pl.ds(start, 1), :]
    for r in range(pairs):
        window = k_high[r].astype(F32) + k_low[r].astype(F32)
        rows = [jnp.zeros((tile_len, wide), F32)] * n_tiles
        for row in range(4):
            rows[(2 * r - 1 + row) % n_tiles] = window[row * tile_len : (row + 1) * tile_len]
        keep(0, r, jnp.concatenate(rows, axis=0) * first[:, r * wide : (r + 1) * wide])

    def slice_step(step, carry):
        old, new = lax.rem(step - 1, 2), lax.rem(step, 2)
        factor = factors[pl.ds(lax.rem(start + step, total_slices), 1), :]
        for r in range(pairs):
            window = slice(r * wide, (r + 2) * wide)
            high = y_high[old, :, window]
            value = dot(high, k_high[r]) + dot(high, k_low[r]) + dot(y_low[old, :, window], k_high[r])
            keep(new, r, value * factor[:, r * wide : (r + 1) * wide])
        return carry

    lax.fori_loop(1, total_slices, slice_step, 0)
    last = (total_slices - 1) % 2
    inner = slice(tile_len, tile_len + order_len)
    product = y_high[last, :, inner].astype(F32) + y_low[last, :, inner].astype(F32)
    col_max = jnp.max(jnp.sum(product, axis=1))
    power = product * (-0.5 / col_max)
    x_full[...] = power
    high, low = split(power)
    x_high[...] = high
    x_low[...] = low

    bands = [slice(r * wide, (r + 1) * wide) for r in range(pairs)]
    second = (y_high.at[0, :, inner], y_low.at[0, :, inner])
    third = (y_high.at[1, :, inner], y_low.at[1, :, inner])

    def product3(left, right, band):
        l_high, l_low = left
        r_high, r_low = right
        return (
            dot(l_high[...], r_high[:, band]) + dot(l_high[...], r_low[:, band]) + dot(l_low[...], r_high[:, band])
        )

    def put(pair, band, value):
        pair[0][:, band], pair[1][:, band] = split(value)

    x = (x_high, x_low)
    for band in bands:
        value = product3(x, x, band)
        put(second, band, value)
        u_full[:, band] = x_full[:, band] + value
    for band in bands:
        value = product3(x, second, band)
        put(third, band, value)
        t_full[:, band] = value
    for band in bands:
        value = product3(third, third, band)
        b_high[:, band] = value.astype(BF16)
        both = t_full[:, band] + value
        t_full[:, band] = both
        second[0][:, band] = both.astype(BF16)
    for band in bands:
        value = dot(b_high[...], second[0][:, band])
        t_full[:, band] += value
        b_low[:, band] = value.astype(BF16)
    for band in bands:
        put(third, band, t_full[:, band] + dot(b_high[...], b_low[:, band]))
        put(x, band, u_full[:, band])
    for band in bands:
        rest = third[0][:, band].astype(F32) + third[1][:, band].astype(F32)
        x_full[:, band] = -(u_full[:, band] + rest + product3(x, third, band))

    base = lax.axis_index("rows") * (width // tile_len) if width < order_len else jnp.int32(0)
    spots = [pl.multiple_of(place(jnp.int32(a)) * tile_len, tile_len) for a in range(n_tiles)]
    for b in range(width // tile_len):
        spot = pl.multiple_of(place(base + b) * tile_len, tile_len)
        columns = slice(b * tile_len, (b + 1) * tile_len)
        for a in range(n_tiles):
            rows = slice(a * tile_len, (a + 1) * tile_len)
            sent[rows, columns] = x_full[pl.ds(spots[a], tile_len), pl.ds(spot, tile_len)]
            mine[rows, columns] = x_full[pl.ds(spot, tile_len), pl.ds(spots[a], tile_len)].T


def per_device(ising_field, bond_sites, hopping, tile_cols):
    slices_here, matrix_order = ising_field.shape
    n_tiles = tile_cols.shape[0]
    tile_len = matrix_order // n_tiles
    bonds = bond_sites.shape[0]
    n_rows = lax.axis_size("rows")
    col_width = matrix_order // n_rows
    total_slices = slices_here * lax.axis_size("tm")
    pairs = n_tiles // 2
    wide = 2 * tile_len
    extended = matrix_order + wide
    vmem = pl.BlockSpec(memory_space=pltpu.VMEM)
    smem = pl.BlockSpec(memory_space=pltpu.SMEM)
    square = (matrix_order, matrix_order)
    field = lax.all_gather(ising_field, "tm", axis=0, tiled=True)
    chunk = 4 * tile_len
    windows = jax.ShapeDtypeStruct((pairs, 2 * wide, wide), BF16)
    k_high, k_low = pl.pallas_call(
        functools.partial(kinetic_kernel, n_tiles, tile_len, 0.5 / total_slices, chunk),
        out_shape=(windows, windows),
        in_specs=[smem, vmem, vmem],
        out_specs=(vmem, vmem),
        scratch_shapes=[
            pltpu.VMEM((extended, chunk), BF16),
            pltpu.VMEM((chunk, matrix_order), BF16),
            pltpu.VMEM((chunk, matrix_order), BF16),
            pltpu.VMEM((pairs, 2 * wide, wide), F32),
        ],
        compiler_params=pltpu.CompilerParams(vmem_limit_bytes=VMEM_BYTES),
        cost_estimate=pl.CostEstimate(
            flops=4 * bonds * 2 * matrix_order * wide, bytes_accessed=4 * matrix_order * wide, transcendentals=0
        ),
        name="kinetic",
    )(tile_cols, bond_sites.T, hopping[None, :])
    width = col_width if col_width % tile_len == 0 else matrix_order
    half = jax.ShapeDtypeStruct((matrix_order, width), F32)
    mine, sent = pl.pallas_call(
        functools.partial(
            green_kernel, n_tiles, tile_len, slices_here, 1.5 / math.sqrt(total_slices), width
        ),
        out_shape=(half, half),
        in_specs=[smem, vmem, vmem, vmem],
        out_specs=(vmem, vmem),
        scratch_shapes=[pltpu.VMEM((total_slices, matrix_order), F32)]
        + [pltpu.VMEM((2, matrix_order, extended), BF16)] * 2
        + [pltpu.VMEM(square, F32)]
        + [pltpu.VMEM(square, BF16)] * 4
        + [pltpu.VMEM(square, F32)] * 2,
        compiler_params=pltpu.CompilerParams(vmem_limit_bytes=VMEM_BYTES),
        cost_estimate=pl.CostEstimate(
            flops=6 * total_slices * matrix_order * 2 * matrix_order * wide + 28 * matrix_order**3,
            bytes_accessed=8 * matrix_order * matrix_order,
            transcendentals=total_slices * matrix_order,
        ),
        name="green",
    )(tile_cols, field, k_high, k_low)
    offset = lax.axis_index("rows") * col_width
    if width != col_width:
        mine = lax.dynamic_slice_in_dim(mine, offset, col_width, 1)
        sent = lax.dynamic_slice_in_dim(sent, offset, col_width, 1)
    n_spin = lax.axis_size("spin")
    other = lax.ppermute(sent, "spin", [(i, n_spin - 1 - i) for i in range(n_spin)])
    row_ids = jnp.arange(matrix_order, dtype=jnp.int32)[:, None]
    col_ids = offset + jnp.arange(col_width, dtype=jnp.int32)[None, :]
    eye_cols = (row_ids == col_ids).astype(F32)
    xcorr = (eye_cols - mine) * other
    return xcorr[None, None]


def solution(mesh):
    placed = (P(("grp", "tm"), None), P(), P(), P())
    return jax.shard_map(
        per_device,
        mesh=mesh,
        in_specs=placed,
        out_specs=P("spin", ("grp", "tm"), None, "rows"),
        check_vma=False,
    )
```

time: 487 us -> 101 us (0.21)
  waiting for transfers between devices: 289 us -> 2.95 us
  Pallas kernels: 0 us -> 78 us
  matrix products: 61.3 us -> 0 us
  other arithmetic: 49.2 us -> 2.47 us
  local copies, waits for them, and re-layouts: 40.3 us -> 2.22 us
  between operations: 14.3 us -> 0.05 us
  blocking collectives: 23.6 us -> 14.9 us
  starting transfers between devices: 8.25 us -> 0.07 us
    all_gather x6 -> x0, waiting for transfers between devices: 209 us -> none  [the longest x4 135 us: per_device(): lax.all_gather(power, 'rows', axis=1, tiled=True)]
    pallas_call x0 -> x2, Pallas kernels: none -> 78 us  [the longest x1 69.1 us: per_device(): pl.pallas_call(functools.partial(green_kernel, n_tiles, tile_len, slices_...]
    ppermute x3 -> x1, waiting for transfers between devices: 79.5 us -> 2.95 us  [per_device(): lax.ppermute(sent, 'spin', [(i, n_spin - 1 - i) for i in range(n_spin)])]
    dot_general x11 -> x0, matrix products: 61.3 us -> none  [the longest x8 45.6 us: matmul_hi(): jnp.dot(left, right, precision=lax.Precision.HIGHEST, preferred_element_t...]
    unnamed x5 -> x0, other arithmetic: 35.9 us -> none
    gather x5 -> x0, local copies, waits for them, and re-layouts: 23 us -> none  [the longest x1 13.4 us: build_kinetic(): kept_mask = tile_mask[site_from // tile_len, site_to // tile_len]]
    all_to_all x1 -> x0, blocking collectives: 18 us -> none  [per_device(): lax.all_to_all(partner, 'rows', split_axis=0, concat_axis=1, tiled=True)]
    all_gather x0 -> x1, blocking collectives: none -> 14.9 us  [per_device(): field = lax.all_gather(ising_field, 'tm', axis=0, tiled=True)]
  transfers between devices with their start and end apart: 9 -> 1, of which waited for: 9 -> 1; matrix products, arithmetic and copies ran while one was open for 2% -> 0% of each run, Pallas kernels for 0% -> 0%
where the time goes in v1:
time: 101 us
  Pallas kernels  78 us (77%)
  blocking collectives  14.9 us (15%)
  waiting for transfers between devices  2.95 us (3%)
  other arithmetic  2.47 us (2%)
  local copies, waits for them, and re-layouts  2.22 us (2%)
    pallas_call x1, Pallas kernels, per_device(): pl.pallas_call(functools.partial(green_kernel, n_tiles, tile_len, slices_...  69.1 us
    all_gather x1, blocking collectives, per_device(): field = lax.all_gather(ising_field, 'tm', axis=0, tiled=True)  14.9 us
    pallas_call x1, Pallas kernels, per_device(): pl.pallas_call(functools.partial(kinetic_kernel, n_tiles, tile_len, 0.5 /...  8.94 us
    ppermute x1, waiting for transfers between devices, per_device(): lax.ppermute(sent, 'spin', [(i, n_spin - 1 - i) for i in range(n_spin)])  2.95 us
    broadcast_in_dim x1, other arithmetic, per_device(): return xcorr[None, None]  2.47 us
    unnamed x6, local copies, waits for them, and re-layouts  2.22 us
  transfers between devices with their start and end apart: 1, of which 1 were waited for; matrix products, arithmetic and copies ran while one was open for 0% of the time, Pallas kernels for 0%

profile of v1, /device:TPU:0, one launch (start us, length us, event | category | flops | bytes accessed | tf_op | source)
XLA Modules:
  0.0 100.7 jit_solution(70792609077420474)
XLA Ops:
  0.0 0.8 copy.8.tile_cols
  0.8 14.9 %all-gather = s32[4,4,768]{2,1,0:T(4,128)S(1)} all-gather(s32[1,4,768]{2,1,0:T(4,128)} %bitcast.7), channel_id=1, replica_groups=mesh['grp'=2,'tm'=4,'spin'=2,'rows'=2] {'tm'}, dimensions={0}, use_global_device_ids=true | all-gather | bytes 61440 | tf_op jit(solution)/shard_map/all_gather | solution.py:222
  15.7 0.0 copy-start
  15.7 0.7 copy-done
  16.5 0.0 copy-start.1
  16.5 0.7 copy-done.1
  17.2 8.9 %kinetic.1 = (bf16[3,512,256]{2,1,0:T(8,128)(2,1)S(1)}, bf16[3,512,256]{2,1,0:T(8,128)(2,1)S(1)}) custom-call(s32[6,3]{1,0:T(8,128)S(1)} %copy.8.tile_cols, s32[2,3072]{1,0:T(2,128)S(1)} %bitcast.5, f32[1,3072]{1,0:T(1,128)S(1)} %bitcast.6), custom_call_target="tpu_custom_call" | custom-call | flops 4831838208 | bytes 786432 | tf_op jit(solution)/shard_map/kinetic/pallas_call | solution.py:225
  26.1 69.1 %green.1 = (f32[768,384]{1,0:T(8,128)S(1)}, f32[768,384]{1,0:T(8,128)S(1)}) custom-call(s32[6,3]{1,0:T(8,128)S(1)} %copy.8.tile_cols, s32[16,768]{1,0:T(8,128)S(1)} %reshape.6.field, bf16[3,512,256]{2,1,0:T(8,128)(2,1)S(1)} %get-tuple-element.9.k_high, bf16[3,512,256]{2,1,0:T(8,128)(2,1)S(1)} %get-tuple-element.10.k_low), custom_call_target="tpu_custom_call" | custom-call | flops 41674604544 | bytes 4718592 | tf_op jit(solution)/shard_map/green/pallas_call | solution.py:244
  95.2 0.1 collective-permute-start
  95.3 2.9 %collective-permute-done = f32[768,384]{1,0:T(8,128)} collective-permute-done((f32[768,384]{1,0:T(8,128)S(1)}, f32[768,384]{1,0:T(8,128)}, u32[]{:S(2)}, u32[]{:S(2)}) %collective-permute-start) | collective-permute-done | bytes 1179680 | tf_op jit(solution)/shard_map/ppermute | solution.py:269
  98.3 2.5 %multiply_bitcast_fusion = f32[1,1,768,384]{3,2,1,0:T(8,128)} fusion(f32[768,384]{1,0:T(8,128)} %collective-permute-done, f32[768,384]{1,0:T(8,128)S(1)} %get-tuple-element.11, s32[384]{0:T(512)S(1)} %iota_add_fusion), kind=kLoop, calls=%fused_computation | loop fusion | flops 1179648 | bytes 3540480 | tf_op jit(solution)/shard_map/broadcast_in_dim | solution.py:274
  (2 shorter events, 0.0 us)
Async XLA Ops:
  15.7 0.7 copy-start
  16.5 0.7 copy-start.1
  95.2 3.0 %collective-permute-start = (f32[768,384]{1,0:T(8,128)S(1)}, f32[768,384]{1,0:T(8,128)}, u32[]{:S(2)}, u32[]{:S(2)}) collective-permute-start(f32[768,384]{1,0:T(8,128)S(1)} %get-tuple-element.12), channel_id=1, source_target_pairs={{0,2},{2,0},{1,3},{3,1},{4,6},{6,4},{5,7},{7,5},{8,10},{10,8},{9,1... | collective-permute-start | bytes 3538952 | tf_op jit(solution)/shard_map/ppermute | solution.py:269

commit v2 on v1

v2 whole, which is shorter than its diff:
```python
import functools
import math

import jax
import jax.numpy as jnp
from jax import lax
from jax.experimental import pallas as pl
from jax.experimental.pallas import tpu as pltpu
from jax.sharding import PartitionSpec as P

BF16 = jnp.bfloat16
F32 = jnp.float32
VMEM_BYTES = 48 * 1024 * 1024


def split(x):
    high = x.astype(BF16)
    return high, (x - high.astype(F32)).astype(BF16)


def dot(left, right):
    return jnp.dot(left, right, preferred_element_type=F32)


def cycle_order(tile_cols, n_tiles):
    order = [jnp.int32(0), tile_cols[1, 0]]
    for _ in range(n_tiles - 2):
        here = order[-1]
        order.append(tile_cols[1, here] + tile_cols[2, here] - order[-2])

    def place(tile):
        found = jnp.int32(0)
        for position, name in enumerate(order):
            found = jnp.where(name == tile, jnp.int32(position), found)
        return found

    return order, place


def kinetic_kernel(
    n_tiles, tile_len, hop_scale, chunk, tile_cols, sites, hopping, k_parts, one_hot, w_high, w_low, total
):
    bonds = sites.shape[1]
    pairs = n_tiles // 2
    wide = 2 * tile_len
    order, _ = cycle_order(tile_cols, n_tiles)
    row_ids = lax.broadcasted_iota(jnp.int32, (tile_len, chunk), 0)
    lane_ids = lax.broadcasted_iota(jnp.int32, (tile_len, tile_len), 1)

    def build(begin, slot):
        site_from = sites[0:1, begin : begin + chunk]
        for p in range(n_tiles):
            hits = jnp.where(row_ids + order[p] * tile_len == site_from, 1.0, 0.0).astype(BF16)
            spots = [p + 1]
            if p == n_tiles - 1:
                spots.append(0)
            if p == 0:
                spots.append(n_tiles + 1)
            for spot in spots:
                one_hot[slot, spot * tile_len : (spot + 1) * tile_len, :] = hits
        for part in range(chunk // tile_len):
            at = slice(begin + part * tile_len, begin + (part + 1) * tile_len)
            inside = slice(part * tile_len, (part + 1) * tile_len)
            site_to = jnp.broadcast_to(sites[1:2, at], (tile_len, tile_len)).T
            weight = jnp.broadcast_to(hopping[0:1, at], (tile_len, tile_len)).T
            high = weight.astype(BF16).astype(F32)
            low = weight - high
            for p in range(n_tiles):
                hit = lane_ids + order[p] * tile_len == site_to
                columns = slice(p * tile_len, (p + 1) * tile_len)
                w_high[slot, inside, columns] = jnp.where(hit, high, 0.0).astype(BF16)
                w_low[slot, inside, columns] = jnp.where(hit, low, 0.0).astype(BF16)

    build(0, 0)
    for begin in range(0, bonds, chunk):
        slot = begin // chunk % 2
        if begin + chunk < bonds:
            build(begin + chunk, 1 - slot)
        for r in range(pairs):
            columns = slice(r * wide, (r + 1) * wide)
            found = one_hot[slot, r * wide : (r + 2) * wide, :]
            weights = jnp.concatenate([w_high[slot, :, columns], w_low[slot, :, columns]], axis=0)
            added = dot(jnp.concatenate([found, found], axis=1), weights)
            total[r] = added if begin == 0 else total[r] + added

    def tile_of(p, q):
        r, half = divmod(q, 2)
        row = (p - (2 * r - 1)) % n_tiles
        return r, slice(row * tile_len, (row + 1) * tile_len), slice(half * tile_len, (half + 1) * tile_len)

    diagonal = lax.broadcasted_iota(jnp.int32, (tile_len, tile_len), 0) == lane_ids
    k_parts[...] = jnp.zeros_like(k_parts)
    for q in range(n_tiles):
        for p in ((q - 1) % n_tiles, q, (q + 1) % n_tiles):
            value = hop_scale * (total[tile_of(p, q)] + total[tile_of(q, p)].T)
            if p == q:
                value = jnp.where(diagonal, 1.0, 0.0) + value
            high, low = split(value)
            r, rows, columns = tile_of(p, q)
            for part, piece in enumerate((high, high, low)):
                k_parts[r, part * 2 * wide + rows.start : part * 2 * wide + rows.stop, columns] = piece


def green_kernel(
    n_tiles, tile_len, coupling, width,
    tile_cols, field, k_parts, mine, sent,
    factors, y_high, y_low, p_high, p_low, a_part, b_part, u_part, p_full, q_full,
):
    total_slices = field.shape[0]
    order_len = n_tiles * tile_len
    pairs = n_tiles // 2
    wide = 2 * tile_len
    order, place = cycle_order(tile_cols, n_tiles)
    strength = (1.0 - 2.0 * lax.axis_index("spin").astype(F32)) * coupling
    for p in range(n_tiles):
        spins_pm = (2 * field[:, pl.ds(pl.multiple_of(order[p] * tile_len, tile_len), tile_len)] - 1).astype(F32)
        factors[:, p * tile_len : (p + 1) * tile_len] = jnp.exp(strength * spins_pm)

    def keep(slot, r, value):
        parts = split(value)
        for ref, part in zip((y_high, y_low), parts):
            ref[slot, :, tile_len + r * wide : tile_len + (r + 1) * wide] = part
            if r == 0:
                ref[slot, :, tile_len + order_len : 2 * tile_len + order_len] = part[:, :tile_len]
            if r == pairs - 1:
                ref[slot, :, :tile_len] = part[:, tile_len:]

    for r in range(pairs):
        window = k_parts[r, : 2 * wide].astype(F32) + k_parts[r, 4 * wide :].astype(F32)
        rows = [jnp.zeros((tile_len, wide), F32)] * n_tiles
        for row in range(4):
            rows[(2 * r - 1 + row) % n_tiles] = window[row * tile_len : (row + 1) * tile_len]
        keep(0, r, jnp.concatenate(rows, axis=0) * factors[0:1, r * wide : (r + 1) * wide])

    def slice_step(step, carry):
        old, new = lax.rem(step - 1, 2), lax.rem(step, 2)
        factor = factors[pl.ds(step, 1), :]
        for r in range(pairs):
            window = slice(r * wide, (r + 2) * wide)
            high = y_high[old, :, window]
            value = dot(jnp.concatenate([high, y_low[old, :, window], high], axis=1), k_parts[r])
            keep(new, r, value * factor[:, r * wide : (r + 1) * wide])
        return carry

    lax.fori_loop(1, total_slices, slice_step, 0)
    last = (total_slices - 1) % 2
    inner = slice(tile_len, tile_len + order_len)
    product = y_high[last, :, inner].astype(F32) + y_low[last, :, inner].astype(F32)
    col_max = jnp.max(jnp.sum(product, axis=1))
    power = product * (0.5 / col_max)
    p_full[...] = power
    high, low = split(power)
    p_high[...] = high
    p_low[...] = low

    bands = [slice(r * wide, (r + 1) * wide) for r in range(pairs)]
    for band in bands:
        value = dot(p_high[...], p_high[:, band])
        a_part[:, band] = value.astype(BF16)
        value -= p_full[:, band]
        q_full[:, band] = value
        u_part[:, band] = value.astype(BF16)
    for band in bands:
        value = -dot(p_high[...], a_part[:, band])
        b_part[:, band] = value.astype(BF16)
    for band in bands:
        value = b_part[:, band].astype(F32) + dot(b_part[...], b_part[:, band])
        q_full[:, band] += value
        a_part[:, band] = value.astype(BF16)
    q_high, q_low = y_high.at[0, :, inner], y_low.at[0, :, inner]
    for band in bands:
        value = -(q_full[:, band] + dot(u_part[...], a_part[:, band]))
        q_full[:, band] = value
        q_high[:, band], q_low[:, band] = split(value)
    for band in bands:
        left = jnp.concatenate([p_high[...], p_low[...], p_high[...]], axis=1)
        right = jnp.concatenate([q_high[:, band], q_high[:, band], q_low[:, band]], axis=0)
        residual = dot(left, right) + (q_full[:, band] - p_full[:, band])
        a_part[:, band] = residual.astype(BF16)
        q_full[:, band] -= residual
    for band in bands:
        q_full[:, band] += dot(q_high[...], a_part[:, band])

    base = lax.axis_index("rows") * (width // tile_len) if width < order_len else jnp.int32(0)
    tile = (tile_len, tile_len)
    diagonal = lax.broadcasted_iota(jnp.int32, tile, 0) == lax.broadcasted_iota(jnp.int32, tile, 1)
    spots = [pl.multiple_of(place(jnp.int32(a)) * tile_len, tile_len) for a in range(n_tiles)]
    for b in range(width // tile_len):
        spot = pl.multiple_of(place(base + b) * tile_len, tile_len)
        columns = slice(b * tile_len, (b + 1) * tile_len)
        for a in range(n_tiles):
            rows = slice(a * tile_len, (a + 1) * tile_len)
            sent[rows, columns] = q_full[pl.ds(spots[a], tile_len), pl.ds(spot, tile_len)]
            unit = jnp.where(diagonal & (base + b == a), 1.0, 0.0)
            mine[rows, columns] = unit - q_full[pl.ds(spot, tile_len), pl.ds(spots[a], tile_len)].T


def per_device(ising_field, bond_sites, hopping, tile_cols):
    slices_here, matrix_order = ising_field.shape
    n_tiles = tile_cols.shape[0]
    tile_len = matrix_order // n_tiles
    bonds = bond_sites.shape[0]
    n_rows = lax.axis_size("rows")
    col_width = matrix_order // n_rows
    total_slices = slices_here * lax.axis_size("tm")
    pairs = n_tiles // 2
    wide = 2 * tile_len
    extended = matrix_order + wide
    vmem = pl.BlockSpec(memory_space=pltpu.VMEM)
    smem = pl.BlockSpec(memory_space=pltpu.SMEM)
    square = (matrix_order, matrix_order)
    n_time = lax.axis_size("tm")
    blocks = [ising_field]
    for ahead in range(1, n_time):
        blocks.append(lax.ppermute(ising_field, "tm", [(i, (i - ahead) % n_time) for i in range(n_time)]))
    field = jnp.concatenate(blocks, axis=0)
    chunk = 4 * tile_len
    k_parts = pl.pallas_call(
        functools.partial(kinetic_kernel, n_tiles, tile_len, 0.5 / total_slices, chunk),
        out_shape=jax.ShapeDtypeStruct((pairs, 6 * wide, wide), BF16),
        in_specs=[smem, vmem, vmem],
        out_specs=vmem,
        scratch_shapes=[
            pltpu.VMEM((2, extended, chunk), BF16),
            pltpu.VMEM((2, chunk, matrix_order), BF16),
            pltpu.VMEM((2, chunk, matrix_order), BF16),
            pltpu.VMEM((pairs, 2 * wide, wide), F32),
        ],
        compiler_params=pltpu.CompilerParams(vmem_limit_bytes=VMEM_BYTES),
        cost_estimate=pl.CostEstimate(
            flops=4 * bonds * 2 * matrix_order * wide, bytes_accessed=4 * matrix_order * wide, transcendentals=0
        ),
        name="kinetic",
    )(tile_cols.T, bond_sites.T, hopping[None, :])
    width = col_width if col_width % tile_len == 0 else matrix_order
    half = jax.ShapeDtypeStruct((matrix_order, width), F32)
    mine, sent = pl.pallas_call(
        functools.partial(
            green_kernel, n_tiles, tile_len, 1.5 / math.sqrt(total_slices), width
        ),
        out_shape=(half, half),
        in_specs=[smem, vmem, vmem],
        out_specs=(vmem, vmem),
        scratch_shapes=[pltpu.VMEM((total_slices, matrix_order), F32)]
        + [pltpu.VMEM((2, matrix_order, extended), BF16)] * 2
        + [pltpu.VMEM(square, BF16)] * 5
        + [pltpu.VMEM(square, F32)] * 2,
        compiler_params=pltpu.CompilerParams(vmem_limit_bytes=VMEM_BYTES),
        cost_estimate=pl.CostEstimate(
            flops=6 * total_slices * matrix_order * 2 * matrix_order * wide + 16 * matrix_order**3,
            bytes_accessed=8 * matrix_order * matrix_order,
            transcendentals=total_slices * matrix_order,
        ),
        name="green",
    )(tile_cols.T, field, k_parts)
    offset = lax.axis_index("rows") * col_width
    if width != col_width:
        mine = lax.dynamic_slice_in_dim(mine, offset, col_width, 1)
        sent = lax.dynamic_slice_in_dim(sent, offset, col_width, 1)
    n_spin = lax.axis_size("spin")
    other = lax.ppermute(sent, "spin", [(i, n_spin - 1 - i) for i in range(n_spin)])
    xcorr = mine * other
    return xcorr[None, None]


def solution(mesh):
    placed = (P(("grp", "tm"), None), P(), P(), P())
    return jax.shard_map(
        per_device,
        mesh=mesh,
        in_specs=placed,
        out_specs=P("spin", ("grp", "tm"), None, "rows"),
        check_vma=False,
    )
```

time: 101 us -> 80.2 us (0.79)
  blocking collectives: 14.9 us -> 0 us
  Pallas kernels: 78 us -> 67.6 us
  starting transfers between devices: 0.07 us -> 6.13 us
  other arithmetic: 2.47 us -> 1.18 us
    all_gather x1 -> x0, blocking collectives: 14.9 us -> none  [per_device(): field = lax.all_gather(ising_field, 'tm', axis=0, tiled=True)]
    pallas_call x1, Pallas kernels: 69.1 us -> 60.6 us  [per_device(): pl.pallas_call(functools.partial(green_kernel, n_tiles, tile_len, 1.5 / m...]
    ppermute x0 -> x3, starting transfers between devices: none -> 6.06 us  [per_device(): lax.ppermute(ising_field, 'tm', [(i, (i - ahead) % n_time) for i in range...]
    pallas_call x1, Pallas kernels: 8.94 us -> 6.94 us  [per_device(): pl.pallas_call(functools.partial(kinetic_kernel, n_tiles, tile_len, 0.5 /...]
    broadcast_in_dim x1, other arithmetic: 2.47 us -> 1.17 us  [per_device(): return xcorr[None, None]]
    unnamed x6 -> x8, local copies, waits for them, and re-layouts: 2.22 us -> 2.13 us
  transfers between devices with their start and end apart: 1 -> 4, of which waited for: 1 -> 1; matrix products, arithmetic and copies ran while one was open for 0% -> 0% of each run, Pallas kernels for 0% -> 9%
where the time goes in v2:
time: 80.2 us; the launch traced here: 79.9 us
  Pallas kernels  67.6 us (84%)
  starting transfers between devices  6.13 us (8%)
  waiting for transfers between devices  2.84 us (4%)
  local copies, waits for them, and re-layouts  2.13 us (3%)
  other arithmetic  1.18 us (1%)
    pallas_call x1, Pallas kernels, per_device(): pl.pallas_call(functools.partial(green_kernel, n_tiles, tile_len, 1.5 / m...  60.6 us
    pallas_call x1, Pallas kernels, per_device(): pl.pallas_call(functools.partial(kinetic_kernel, n_tiles, tile_len, 0.5 /...  6.94 us
    ppermute x3, starting transfers between devices, per_device(): lax.ppermute(ising_field, 'tm', [(i, (i - ahead) % n_time) for i in range...  6.06 us
    ppermute x1, waiting for transfers between devices, per_device(): lax.ppermute(sent, 'spin', [(i, n_spin - 1 - i) for i in range(n_spin)])  2.83 us
    unnamed x8, local copies, waits for them, and re-layouts  2.13 us
  transfers between devices with their start and end apart: 4, of which 1 were waited for; matrix products, arithmetic and copies ran while one was open for 0% of the time, Pallas kernels for 9%

profile of v2, /device:TPU:0, one launch (start us, length us, event | category | flops | bytes accessed | tf_op | source)
XLA Modules:
  0.0 79.9 jit_solution(544260766120440962)
XLA Ops:
  0.0 4.0 %collective-permute-start.1 = (s32[4,768]{1,0:T(4,128)}, s32[4,768]{1,0:T(4,128)S(1)}, u32[]{:S(2)}, u32[]{:S(2)}) collective-permute-start(s32[4,768]{1,0:T(4,128)} %param.4), channel_id=1, source_target_pairs={{0,8},{4,12},{8,0},{12,4},{1,9},{5,13},{9,1},{13,5},{2,10},{6,14},... | collective-permute-start | bytes 36872 | tf_op jit(solution)/shard_map/ppermute | solution.py:215
  4.0 1.3 %collective-permute-start = (s32[4,768]{1,0:T(4,128)}, s32[4,768]{1,0:T(4,128)S(1)}, u32[]{:S(2)}, u32[]{:S(2)}) collective-permute-start(s32[4,768]{1,0:T(4,128)} %param.4), channel_id=1, source_target_pairs={{0,12},{4,0},{8,4},{12,8},{1,13},{5,1},{9,5},{13,9},{2,14},{6,2},{... | collective-permute-start | bytes 36872 | tf_op jit(solution)/shard_map/ppermute | solution.py:215
  5.4 0.7 collective-permute-start.2
  6.1 0.0 copy-start
  6.1 0.7 copy-done
  6.8 0.0 copy-start.1
  6.8 0.7 copy-done.1
  7.5 0.0 copy-start.2
  7.5 0.7 copy-done.2
  8.2 0.0 copy-start.3
  8.2 6.9 %kinetic.1.k_parts = bf16[3,1536,256]{2,1,0:T(8,128)(2,1)S(1)} custom-call(s32[3,6]{1,0:T(4,128)S(1)} %bitcast.7, s32[2,3072]{1,0:T(2,128)S(1)} %bitcast.5, f32[1,3072]{1,0:T(1,128)S(1)} %bitcast.6), custom_call_target="tpu_custom_call" | custom-call | flops 4831838208 | bytes 786432 | tf_op jit(solution)/shard_map/kinetic/pallas_call | solution.py:218
  15.1 0.0 collective-permute-done.1
  15.2 0.0 collective-permute-done
  15.2 0.0 collective-permute-done.2
  15.2 0.0 copy-done.3
  15.2 60.6 %green.1 = (f32[768,384]{1,0:T(8,128)S(1)}, f32[768,384]{1,0:T(8,128)S(1)}) custom-call(s32[3,6]{1,0:T(4,128)S(1)} %bitcast.8, s32[16,768]{1,0:T(8,128)S(1)} %pad_add_fusion.field, bf16[3,1536,256]{2,1,0:T(8,128)(2,1)S(1)} %kinetic.1.k_parts), custom_call_target="tpu_custom_call" | custom-call | flops 36238786560 | bytes 4718592 | tf_op jit(solution)/shard_map/green/pallas_call | solution.py:237
  75.8 0.1 collective-permute-start.3
  75.9 2.8 %collective-permute-done.3 = f32[768,384]{1,0:T(8,128)S(1)} collective-permute-done((f32[768,384]{1,0:T(8,128)S(1)}, f32[768,384]{1,0:T(8,128)S(1)}, u32[]{:S(2)}, u32[]{:S(2)}) %collective-permute-start.3) | collective-permute-done | bytes 1179680 | tf_op jit(solution)/shard_map/ppermute | solution.py:261
  78.7 1.2 %multiply_bitcast_fusion = f32[1,1,768,384]{3,2,1,0:T(8,128)} fusion(f32[768,384]{1,0:T(8,128)S(1)} %get-tuple-element.7, f32[768,384]{1,0:T(8,128)S(1)} %collective-permute-done.3), kind=kLoop, calls=%fused_computation | loop fusion | flops 294912 | bytes 3538944 | tf_op jit(solution)/shard_map/broadcast_in_dim | solution.py:263
  (1 shorter events, 0.0 us)
Async XLA Ops:
  0.0 15.1 %collective-permute-start.1 = (s32[4,768]{1,0:T(4,128)}, s32[4,768]{1,0:T(4,128)S(1)}, u32[]{:S(2)}, u32[]{:S(2)}) collective-permute-start(s32[4,768]{1,0:T(4,128)} %param.4), channel_id=1, source_target_pairs={{0,8},{4,12},{8,0},{12,4},{1,9},{5,13},{9,1},{13,5},{2,10},{6,14},... | collective-permute-start | bytes 36872 | tf_op jit(solution)/shard_map/ppermute | solution.py:215
  4.0 11.1 %collective-permute-start = (s32[4,768]{1,0:T(4,128)}, s32[4,768]{1,0:T(4,128)S(1)}, u32[]{:S(2)}, u32[]{:S(2)}) collective-permute-start(s32[4,768]{1,0:T(4,128)} %param.4), channel_id=1, source_target_pairs={{0,12},{4,0},{8,4},{12,8},{1,13},{5,1},{9,5},{13,9},{2,14},{6,2},{... | collective-permute-start | bytes 36872 | tf_op jit(solution)/shard_map/ppermute | solution.py:215
  5.4 9.8 %collective-permute-start.2 = (s32[4,768]{1,0:T(4,128)}, s32[4,768]{1,0:T(4,128)S(1)}, u32[]{:S(2)}, u32[]{:S(2)}) collective-permute-start(s32[4,768]{1,0:T(4,128)} %param.4), channel_id=1, source_target_pairs={{0,4},{4,8},{8,12},{12,0},{1,5},{5,9},{9,13},{13,1},{2,6},{6,10},{... | collective-permute-start | bytes 36872 | tf_op jit(solution)/shard_map/ppermute | solution.py:215
  6.1 0.7 copy-start
  6.8 0.7 copy-start.1
  7.5 0.7 copy-start.2
  8.2 7.0 %copy-start.3 = (s32[4,768]{1,0:T(4,128)S(1)}, s32[4,768]{1,0:T(4,128)}, u32[]{:S(2)}) copy-start(s32[4,768]{1,0:T(4,128)} %param.4) | copy-start | bytes 36868
  75.8 2.9 %collective-permute-start.3 = (f32[768,384]{1,0:T(8,128)S(1)}, f32[768,384]{1,0:T(8,128)S(1)}, u32[]{:S(2)}, u32[]{:S(2)}) collective-permute-start(f32[768,384]{1,0:T(8,128)S(1)} %get-tuple-element.8), channel_id=1, source_target_pairs={{0,2},{2,0},{1,3},{3,1},{4,6},{6,4},{5,7},{7,5},{8,10},{10,8},{9,1... | collective-permute-start | bytes 3538952 | tf_op jit(solution)/shard_map/ppermute | solution.py:261

commit v3 on v2

--- a/solution.py
+++ b/solution.py
@@ -104,7 +104,7 @@
 def green_kernel(
     n_tiles, tile_len, coupling, width,
     tile_cols, field, k_parts, mine, sent,
-    factors, y_high, y_low, p_high, p_low, a_part, b_part, u_part, p_full, q_full,
+    factors, even_high, even_low, odd_high, odd_low, p_high, p_low, a_part, b_part, u_part, p_full, q_full,
 ):
     total_slices = field.shape[0]
     order_len = n_tiles * tile_len
@@ -116,36 +116,48 @@
         spins_pm = (2 * field[:, pl.ds(pl.multiple_of(order[p] * tile_len, tile_len), tile_len)] - 1).astype(F32)
         factors[:, p * tile_len : (p + 1) * tile_len] = jnp.exp(strength * spins_pm)
 
-    def keep(slot, r, value):
+    even, odd = (even_high, even_low), (odd_high, odd_low)
+
+    def keep(refs, r, value):
         parts = split(value)
-        for ref, part in zip((y_high, y_low), parts):
-            ref[slot, :, tile_len + r * wide : tile_len + (r + 1) * wide] = part
+        for ref, part in zip(refs, parts):
+            ref[:, tile_len + r * wide : tile_len + (r + 1) * wide] = part
             if r == 0:
-                ref[slot, :, tile_len + order_len : 2 * tile_len + order_len] = part[:, :tile_len]
+                ref[:, tile_len + order_len : 2 * tile_len + order_len] = part[:, :tile_len]
             if r == pairs - 1:
-                ref[slot, :, :tile_len] = part[:, tile_len:]
+                ref[:, :tile_len] = part[:, tile_len:]
 
     for r in range(pairs):
         window = k_parts[r, : 2 * wide].astype(F32) + k_parts[r, 4 * wide :].astype(F32)
         rows = [jnp.zeros((tile_len, wide), F32)] * n_tiles
         for row in range(4):
             rows[(2 * r - 1 + row) % n_tiles] = window[row * tile_len : (row + 1) * tile_len]
-        keep(0, r, jnp.concatenate(rows, axis=0) * factors[0:1, r * wide : (r + 1) * wide])
-
-    def slice_step(step, carry):
-        old, new = lax.rem(step - 1, 2), lax.rem(step, 2)
-        factor = factors[pl.ds(step, 1), :]
-        for r in range(pairs):
-            window = slice(r * wide, (r + 2) * wide)
-            high = y_high[old, :, window]
-            value = dot(jnp.concatenate([high, y_low[old, :, window], high], axis=1), k_parts[r])
-            keep(new, r, value * factor[:, r * wide : (r + 1) * wide])
+        keep(even, r, jnp.concatenate(rows, axis=0) * factors[0:1, r * wide : (r + 1) * wide])
+
+    def multiplied(refs, step, r):
+        window = slice(r * wide, (r + 2) * wide)
+        high = refs[0][:, window]
+        value = dot(jnp.concatenate([high, refs[1][:, window], high], axis=1), k_parts[r])
+        return value * factors[pl.ds(step, 1), r * wide : (r + 1) * wide]
+
+    def two_steps(pair, carry):
+        step = 2 * pair + 1
+        for r in range(pairs):
+            keep(odd, r, multiplied(even, step, r))
+        for r in range(pairs):
+            keep(even, r, multiplied(odd, step + 1, r))
         return carry
 
-    lax.fori_loop(1, total_slices, slice_step, 0)
-    last = (total_slices - 1) % 2
+    lax.fori_loop(0, (total_slices - 2) // 2, two_steps, 0)
+    newest = even
+    if total_slices % 2:
+        for r in range(pairs):
+            keep(odd, r, multiplied(even, total_slices - 2, r))
+        newest = odd
+    for r in range(pairs):
+        p_full[:, r * wide : (r + 1) * wide] = multiplied(newest, total_slices - 1, r)
     inner = slice(tile_len, tile_len + order_len)
-    product = y_high[last, :, inner].astype(F32) + y_low[last, :, inner].astype(F32)
+    product = p_full[...]
     col_max = jnp.max(jnp.sum(product, axis=1))
     power = product * (0.5 / col_max)
     p_full[...] = power
@@ -167,7 +179,7 @@
         value = b_part[:, band].astype(F32) + dot(b_part[...], b_part[:, band])
         q_full[:, band] += value
         a_part[:, band] = value.astype(BF16)
-    q_high, q_low = y_high.at[0, :, inner], y_low.at[0, :, inner]
+    q_high, q_low = even_high.at[:, inner], even_low.at[:, inner]
     for band in bands:
         value = -(q_full[:, band] + dot(u_part[...], a_part[:, band]))
         q_full[:, band] = value
@@ -242,7 +254,7 @@
         in_specs=[smem, vmem, vmem],
         out_specs=(vmem, vmem),
         scratch_shapes=[pltpu.VMEM((total_slices, matrix_order), F32)]
-        + [pltpu.VMEM((2, matrix_order, extended), BF16)] * 2
+        + [pltpu.VMEM((matrix_order, extended), BF16)] * 4
         + [pltpu.VMEM(square, BF16)] * 5
         + [pltpu.VMEM(square, F32)] * 2,
         compiler_params=pltpu.CompilerParams(vmem_limit_bytes=VMEM_BYTES),

time: 80.2 us -> 69.3 us (0.86)
  Pallas kernels: 67.6 us -> 56.7 us
    pallas_call x1, Pallas kernels: 60.6 us -> 49.7 us  [per_device(): pl.pallas_call(functools.partial(green_kernel, n_tiles, tile_len, 1.5 / m...]
  transfers between devices with their start and end apart: 4 -> 4, of which waited for: 1 -> 1; matrix products, arithmetic and copies ran while one was open for 0% -> 0% of each run, Pallas kernels for 9% -> 10%
where the time goes in v3:
time: 69.3 us; the launch traced here: 69 us
  Pallas kernels  56.7 us (82%)
  starting transfers between devices  6.13 us (9%)
  waiting for transfers between devices  2.84 us (4%)
  local copies, waits for them, and re-layouts  2.13 us (3%)
  other arithmetic  1.18 us (2%)
    pallas_call x1, Pallas kernels, per_device(): pl.pallas_call(functools.partial(green_kernel, n_tiles, tile_len, 1.5 / m...  49.7 us
    pallas_call x1, Pallas kernels, per_device(): pl.pallas_call(functools.partial(kinetic_kernel, n_tiles, tile_len, 0.5 /...  6.94 us
    ppermute x3, starting transfers between devices, per_device(): lax.ppermute(ising_field, 'tm', [(i, (i - ahead) % n_time) for i in range...  6.06 us
    ppermute x1, waiting for transfers between devices, per_device(): lax.ppermute(sent, 'spin', [(i, n_spin - 1 - i) for i in range(n_spin)])  2.83 us
    unnamed x8, local copies, waits for them, and re-layouts  2.13 us
  transfers between devices with their start and end apart: 4, of which 1 were waited for; matrix products, arithmetic and copies ran while one was open for 0% of the time, Pallas kernels for 10%

profile of v3, /device:TPU:0, one launch (start us, length us, event | category | flops | bytes accessed | tf_op | source)
XLA Modules:
  0.0 69.0 jit_solution(13048992716749715394)
XLA Ops:
  0.0 4.0 %collective-permute-start.1 = (s32[4,768]{1,0:T(4,128)}, s32[4,768]{1,0:T(4,128)S(1)}, u32[]{:S(2)}, u32[]{:S(2)}) collective-permute-start(s32[4,768]{1,0:T(4,128)} %param.4), channel_id=1, source_target_pairs={{0,8},{4,12},{8,0},{12,4},{1,9},{5,13},{9,1},{13,5},{2,10},{6,14},... | collective-permute-start | bytes 36872 | tf_op jit(solution)/shard_map/ppermute | solution.py:227
  4.0 1.3 %collective-permute-start = (s32[4,768]{1,0:T(4,128)}, s32[4,768]{1,0:T(4,128)S(1)}, u32[]{:S(2)}, u32[]{:S(2)}) collective-permute-start(s32[4,768]{1,0:T(4,128)} %param.4), channel_id=1, source_target_pairs={{0,12},{4,0},{8,4},{12,8},{1,13},{5,1},{9,5},{13,9},{2,14},{6,2},{... | collective-permute-start | bytes 36872 | tf_op jit(solution)/shard_map/ppermute | solution.py:227
  5.4 0.7 collective-permute-start.2
  6.1 0.0 copy-start
  6.1 0.7 %copy-done = s32[3072,2]{0,1:T(2,128)S(1)} copy-done((s32[3072,2]{0,1:T(2,128)S(1)}, s32[3072,2]{0,1:T(2,128)}, u32[]{:S(2)}) %copy-start) | copy-done | bytes 24600
  6.8 0.0 copy-start.1
  6.8 0.7 %copy-done.1 = f32[3072]{0:T(1024)S(1)} copy-done((f32[3072]{0:T(1024)S(1)}, f32[3072]{0:T(1024)}, u32[]{:S(2)}) %copy-start.1) | copy-done | bytes 12312
  7.5 0.0 copy-start.2
  7.5 0.7 copy-done.2
  8.2 0.0 copy-start.3
  8.2 6.9 %kinetic.1.k_parts = bf16[3,1536,256]{2,1,0:T(8,128)(2,1)S(1)} custom-call(s32[3,6]{1,0:T(4,128)S(1)} %bitcast.7, s32[2,3072]{1,0:T(2,128)S(1)} %bitcast.5, f32[1,3072]{1,0:T(1,128)S(1)} %bitcast.6), custom_call_target="tpu_custom_call" | custom-call | flops 4831838208 | bytes 786432 | tf_op jit(solution)/shard_map/kinetic/pallas_call | solution.py:230
  15.1 0.0 collective-permute-done.1
  15.2 0.0 collective-permute-done
  15.2 0.0 collective-permute-done.2
  15.2 0.0 copy-done.3
  15.2 49.7 %green.1 = (f32[768,384]{1,0:T(8,128)S(1)}, f32[768,384]{1,0:T(8,128)S(1)}) custom-call(s32[3,6]{1,0:T(4,128)S(1)} %bitcast.8, s32[16,768]{1,0:T(8,128)S(1)} %pad_add_fusion.field, bf16[3,1536,256]{2,1,0:T(8,128)(2,1)S(1)} %kinetic.1.k_parts), custom_call_target="tpu_custom_call" | custom-call | flops 36238786560 | bytes 4718592 | tf_op jit(solution)/shard_map/green/pallas_call | solution.py:249
  64.9 0.1 collective-permute-start.3
  65.0 2.8 %collective-permute-done.3 = f32[768,384]{1,0:T(8,128)S(1)} collective-permute-done((f32[768,384]{1,0:T(8,128)S(1)}, f32[768,384]{1,0:T(8,128)S(1)}, u32[]{:S(2)}, u32[]{:S(2)}) %collective-permute-start.3) | collective-permute-done | bytes 1179680 | tf_op jit(solution)/shard_map/ppermute | solution.py:273
  67.8 1.2 %multiply_bitcast_fusion = f32[1,1,768,384]{3,2,1,0:T(8,128)} fusion(f32[768,384]{1,0:T(8,128)S(1)} %get-tuple-element.7, f32[768,384]{1,0:T(8,128)S(1)} %collective-permute-done.3), kind=kLoop, calls=%fused_computation | loop fusion | flops 294912 | bytes 3538944 | tf_op jit(solution)/shard_map/broadcast_in_dim | solution.py:275
  (1 shorter events, 0.0 us)
Async XLA Ops:
  0.0 15.1 %collective-permute-start.1 = (s32[4,768]{1,0:T(4,128)}, s32[4,768]{1,0:T(4,128)S(1)}, u32[]{:S(2)}, u32[]{:S(2)}) collective-permute-start(s32[4,768]{1,0:T(4,128)} %param.4), channel_id=1, source_target_pairs={{0,8},{4,12},{8,0},{12,4},{1,9},{5,13},{9,1},{13,5},{2,10},{6,14},... | collective-permute-start | bytes 36872 | tf_op jit(solution)/shard_map/ppermute | solution.py:227
  4.0 11.1 %collective-permute-start = (s32[4,768]{1,0:T(4,128)}, s32[4,768]{1,0:T(4,128)S(1)}, u32[]{:S(2)}, u32[]{:S(2)}) collective-permute-start(s32[4,768]{1,0:T(4,128)} %param.4), channel_id=1, source_target_pairs={{0,12},{4,0},{8,4},{12,8},{1,13},{5,1},{9,5},{13,9},{2,14},{6,2},{... | collective-permute-start | bytes 36872 | tf_op jit(solution)/shard_map/ppermute | solution.py:227
  5.4 9.8 %collective-permute-start.2 = (s32[4,768]{1,0:T(4,128)}, s32[4,768]{1,0:T(4,128)S(1)}, u32[]{:S(2)}, u32[]{:S(2)}) collective-permute-start(s32[4,768]{1,0:T(4,128)} %param.4), channel_id=1, source_target_pairs={{0,4},{4,8},{8,12},{12,0},{1,5},{5,9},{9,13},{13,1},{2,6},{6,10},{... | collective-permute-start | bytes 36872 | tf_op jit(solution)/shard_map/ppermute | solution.py:227
  6.1 0.7 %copy-start = (s32[3072,2]{0,1:T(2,128)S(1)}, s32[3072,2]{0,1:T(2,128)}, u32[]{:S(2)}) copy-start(s32[3072,2]{0,1:T(2,128)} %param.5) | copy-start | bytes 73732
  6.8 0.7 %copy-start.1 = (f32[3072]{0:T(1024)S(1)}, f32[3072]{0:T(1024)}, u32[]{:S(2)}) copy-start(f32[3072]{0:T(1024)} %param.6) | copy-start | bytes 36868
  7.5 0.7 copy-start.2
  8.2 7.0 %copy-start.3 = (s32[4,768]{1,0:T(4,128)S(1)}, s32[4,768]{1,0:T(4,128)}, u32[]{:S(2)}) copy-start(s32[4,768]{1,0:T(4,128)} %param.4) | copy-start | bytes 36868
  64.9 2.9 %collective-permute-start.3 = (f32[768,384]{1,0:T(8,128)S(1)}, f32[768,384]{1,0:T(8,128)S(1)}, u32[]{:S(2)}, u32[]{:S(2)}) collective-permute-start(f32[768,384]{1,0:T(8,128)S(1)} %get-tuple-element.8), channel_id=1, source_target_pairs={{0,2},{2,0},{1,3},{3,1},{4,6},{6,4},{5,7},{7,5},{8,10},{10,8},{9,1... | collective-permute-start | bytes 3538952 | tf_op jit(solution)/shard_map/ppermute | solution.py:273

commit v4 on v3

--- a/solution.py
+++ b/solution.py
@@ -11,6 +11,7 @@
 BF16 = jnp.bfloat16
 F32 = jnp.float32
 VMEM_BYTES = 48 * 1024 * 1024
+MESH = pl.DeviceIdType.MESH
 
 
 def split(x):
@@ -38,8 +39,14 @@
 
 
 def kinetic_kernel(
-    n_tiles, tile_len, hop_scale, chunk, tile_cols, sites, hopping, k_parts, one_hot, w_high, w_low, total
+    n_tiles, tile_len, hop_scale, chunk, n_time, tile_cols, sites, hopping, field, k_parts, circle,
+    one_hot, w_high, w_low, total, landed, send_sems, recv_sems
 ):
+    me = lax.axis_index("tm")
+    barrier = pltpu.get_barrier_semaphore()
+    for ahead in range(1, n_time):
+        peer = lax.rem(me + ahead, n_time)
+        pl.semaphore_signal(barrier, inc=1, device_id={"tm": peer}, device_id_type=MESH)
     bonds = sites.shape[1]
     pairs = n_tiles // 2
     wide = 2 * tile_len
@@ -72,7 +79,22 @@
                 w_low[slot, inside, columns] = jnp.where(hit, low, 0.0).astype(BF16)
 
     build(0, 0)
+    copies = []
     for begin in range(0, bonds, chunk):
+        if begin == chunk:
+            pl.semaphore_wait(barrier, n_time - 1)
+            for ahead in range(1, n_time):
+                copies.append(
+                    pltpu.make_async_remote_copy(
+                        src_ref=field,
+                        dst_ref=landed.at[ahead],
+                        send_sem=send_sems.at[ahead],
+                        recv_sem=recv_sems.at[ahead],
+                        device_id={"tm": lax.rem(me + n_time - ahead, n_time)},
+                        device_id_type=MESH,
+                    )
+                )
+                copies[-1].start()
         slot = begin // chunk % 2
         if begin + chunk < bonds:
             build(begin + chunk, 1 - slot)
@@ -99,6 +121,12 @@
             r, rows, columns = tile_of(p, q)
             for part, piece in enumerate((high, high, low)):
                 k_parts[r, part * 2 * wide + rows.start : part * 2 * wide + rows.stop, columns] = piece
+    for copy in copies:
+        copy.wait()
+    slices_here = field.shape[0]
+    for ahead in range(n_time):
+        block = field[...] if ahead == 0 else landed[ahead]
+        circle[ahead * slices_here : (ahead + 1) * slices_here, :] = block
 
 
 def green_kernel(
@@ -222,28 +250,32 @@
     smem = pl.BlockSpec(memory_space=pltpu.SMEM)
     square = (matrix_order, matrix_order)
     n_time = lax.axis_size("tm")
-    blocks = [ising_field]
-    for ahead in range(1, n_time):
-        blocks.append(lax.ppermute(ising_field, "tm", [(i, (i - ahead) % n_time) for i in range(n_time)]))
-    field = jnp.concatenate(blocks, axis=0)
     chunk = 4 * tile_len
-    k_parts = pl.pallas_call(
-        functools.partial(kinetic_kernel, n_tiles, tile_len, 0.5 / total_slices, chunk),
-        out_shape=jax.ShapeDtypeStruct((pairs, 6 * wide, wide), BF16),
-        in_specs=[smem, vmem, vmem],
-        out_specs=vmem,
+    k_parts, circle = pl.pallas_call(
+        functools.partial(kinetic_kernel, n_tiles, tile_len, 0.5 / total_slices, chunk, n_time),
+        out_shape=(
+            jax.ShapeDtypeStruct((pairs, 6 * wide, wide), BF16),
+            jax.ShapeDtypeStruct((total_slices, matrix_order), jnp.int32),
+        ),
+        in_specs=[smem, vmem, vmem, vmem],
+        out_specs=(vmem, vmem),
         scratch_shapes=[
             pltpu.VMEM((2, extended, chunk), BF16),
             pltpu.VMEM((2, chunk, matrix_order), BF16),
             pltpu.VMEM((2, chunk, matrix_order), BF16),
             pltpu.VMEM((pairs, 2 * wide, wide), F32),
+            pltpu.VMEM((n_time, slices_here, matrix_order), jnp.int32),
+            pltpu.SemaphoreType.DMA((n_time,)),
+            pltpu.SemaphoreType.DMA((n_time,)),
         ],
-        compiler_params=pltpu.CompilerParams(vmem_limit_bytes=VMEM_BYTES),
+        compiler_params=pltpu.CompilerParams(
+            vmem_limit_bytes=VMEM_BYTES, collective_id=0, has_side_effects=True
+        ),
         cost_estimate=pl.CostEstimate(
             flops=4 * bonds * 2 * matrix_order * wide, bytes_accessed=4 * matrix_order * wide, transcendentals=0
         ),
         name="kinetic",
-    )(tile_cols.T, bond_sites.T, hopping[None, :])
+    )(tile_cols.T, bond_sites.T, hopping[None, :], ising_field)
     width = col_width if col_width % tile_len == 0 else matrix_order
     half = jax.ShapeDtypeStruct((matrix_order, width), F32)
     mine, sent = pl.pallas_call(
@@ -264,7 +296,7 @@
             transcendentals=total_slices * matrix_order,
         ),
         name="green",
-    )(tile_cols.T, field, k_parts)
+    )(tile_cols.T, circle, k_parts)
     offset = lax.axis_index("rows") * col_width
     if width != col_width:
         mine = lax.dynamic_slice_in_dim(mine, offset, col_width, 1)

time: 69.3 us -> 68.5 us (0.988)
  starting transfers between devices: 6.13 us -> 0.07 us
  Pallas kernels: 56.7 us -> 61.2 us
  local copies, waits for them, and re-layouts: 2.13 us -> 2.83 us
    ppermute x3 -> x0, starting transfers between devices: 6.06 us -> none  [per_device(): lax.ppermute(ising_field, 'tm', [(i, (i - ahead) % n_time) for i in range...]
    pallas_call x1, Pallas kernels: 6.94 us -> 11.5 us  [per_device(): pl.pallas_call(functools.partial(kinetic_kernel, n_tiles, tile_len, 0.5 /...]
    unnamed x8, local copies, waits for them, and re-layouts: 2.13 us -> 2.83 us
  transfers between devices with their start and end apart: 4 -> 1, of which waited for: 1 -> 1; matrix products, arithmetic and copies ran while one was open for 0% -> 0% of each run, Pallas kernels for 10% -> 0%
where the time goes in v4:
time: 68.5 us; the launch traced here: 68.1 us
  Pallas kernels  61.2 us (89%)
  local copies, waits for them, and re-layouts  2.83 us (4%)
  waiting for transfers between devices  2.83 us (4%)
  other arithmetic  1.17 us (2%)
    pallas_call x1, Pallas kernels, per_device(): pl.pallas_call(functools.partial(green_kernel, n_tiles, tile_len, 1.5 / m...  49.7 us
    pallas_call x1, Pallas kernels, per_device(): pl.pallas_call(functools.partial(kinetic_kernel, n_tiles, tile_len, 0.5 /...  11.5 us
    ppermute x1, waiting for transfers between devices, per_device(): lax.ppermute(sent, 'spin', [(i, n_spin - 1 - i) for i in range(n_spin)])  2.83 us
    unnamed x8, local copies, waits for them, and re-layouts  2.83 us
  transfers between devices with their start and end apart: 1, of which 1 were waited for; matrix products, arithmetic and copies ran while one was open for 0% of the time, Pallas kernels for 0%

profile of v4, /device:TPU:0, one launch (start us, length us, event | category | flops | bytes accessed | tf_op | source)
XLA Modules:
  0.0 68.1 jit_solution(11367059174790784838)
XLA Ops:
  0.0 0.0 copy-start
  0.0 0.7 %copy-done = s32[3072,2]{0,1:T(2,128)S(1)} copy-done((s32[3072,2]{0,1:T(2,128)S(1)}, s32[3072,2]{0,1:T(2,128)}, u32[]{:S(2)}) %copy-start) | copy-done | bytes 24600
  0.7 0.0 copy-start.1
  0.7 0.7 %copy-done.1 = f32[3072]{0:T(1024)S(1)} copy-done((f32[3072]{0:T(1024)S(1)}, f32[3072]{0:T(1024)}, u32[]{:S(2)}) %copy-start.1) | copy-done | bytes 12312
  1.4 0.0 copy-start.2
  1.4 0.7 %copy-done.2 = s32[4,768]{1,0:T(4,128)S(1)} copy-done((s32[4,768]{1,0:T(4,128)S(1)}, s32[4,768]{1,0:T(4,128)}, u32[]{:S(2)}) %copy-start.2) | copy-done | bytes 12312
  2.2 0.0 copy-start.3
  2.2 0.7 copy-done.3
  2.8 11.5 %kinetic.1 = (bf16[3,1536,256]{2,1,0:T(8,128)(2,1)S(1)}, s32[16,768]{1,0:T(8,128)S(1)}) custom-call(s32[3,6]{1,0:T(4,128)S(1)} %bitcast.7, s32[2,3072]{1,0:T(2,128)S(1)} %bitcast.5, f32[1,3072]{1,0:T(1,128)S(1)} %bitcast.6, s32[4,768]{1,0:T(4,128)S(1)} %copy-done.2), custom_call_target="tpu_custom_call" | custom-call | flops 4831838208 | bytes 786432 | tf_op jit(solution)/shard_map/kinetic/pallas_call | solution.py:254
  14.3 49.7 %green.1 = (f32[768,384]{1,0:T(8,128)S(1)}, f32[768,384]{1,0:T(8,128)S(1)}) custom-call(s32[3,6]{1,0:T(4,128)S(1)} %bitcast.8, s32[16,768]{1,0:T(8,128)S(1)} %get-tuple-element.9.field, bf16[3,1536,256]{2,1,0:T(8,128)(2,1)S(1)} %get-tuple-element.10.k_parts), custom_call_target="tpu_custom_call" | custom-call | flops 36238786560 | bytes 4718592 | tf_op jit(solution)/shard_map/green/pallas_call | solution.py:281
  64.1 0.1 collective-permute-start
  64.1 2.8 %collective-permute-done = f32[768,384]{1,0:T(8,128)S(1)} collective-permute-done((f32[768,384]{1,0:T(8,128)S(1)}, f32[768,384]{1,0:T(8,128)S(1)}, u32[]{:S(2)}, u32[]{:S(2)}) %collective-permute-start) | collective-permute-done | bytes 1179680 | tf_op jit(solution)/shard_map/ppermute | solution.py:305
  67.0 1.2 %multiply_bitcast_fusion = f32[1,1,768,384]{3,2,1,0:T(8,128)} fusion(f32[768,384]{1,0:T(8,128)S(1)} %get-tuple-element.11, f32[768,384]{1,0:T(8,128)S(1)} %collective-permute-done), kind=kLoop, calls=%fused_computation | loop fusion | flops 294912 | bytes 3538944 | tf_op jit(solution)/shard_map/broadcast_in_dim | solution.py:307
Async XLA Ops:
  0.0 0.7 %copy-start = (s32[3072,2]{0,1:T(2,128)S(1)}, s32[3072,2]{0,1:T(2,128)}, u32[]{:S(2)}) copy-start(s32[3072,2]{0,1:T(2,128)} %param.5) | copy-start | bytes 73732
  0.7 0.7 %copy-start.1 = (f32[3072]{0:T(1024)S(1)}, f32[3072]{0:T(1024)}, u32[]{:S(2)}) copy-start(f32[3072]{0:T(1024)} %param.6) | copy-start | bytes 36868
  1.4 0.7 %copy-start.2 = (s32[4,768]{1,0:T(4,128)S(1)}, s32[4,768]{1,0:T(4,128)}, u32[]{:S(2)}) copy-start(s32[4,768]{1,0:T(4,128)} %field.1) | copy-start | bytes 36868
  2.2 0.7 %copy-start.3 = (s32[6,3]{0,1:T(4,128)S(1)}, s32[6,3]{0,1:T(4,128)}, u32[]{:S(2)}) copy-start(s32[6,3]{0,1:T(4,128)} %param.7) | copy-start | bytes 220
  64.1 2.9 %collective-permute-start = (f32[768,384]{1,0:T(8,128)S(1)}, f32[768,384]{1,0:T(8,128)S(1)}, u32[]{:S(2)}, u32[]{:S(2)}) collective-permute-start(f32[768,384]{1,0:T(8,128)S(1)} %get-tuple-element.12), channel_id=1, source_target_pairs={{0,2},{2,0},{1,3},{3,1},{4,6},{6,4},{5,7},{7,5},{8,10},{10,8},{9,1... | collective-permute-start | bytes 3538952 | tf_op jit(solution)/shard_map/ppermute | solution.py:305

commit v5 on v4

--- a/solution.py
+++ b/solution.py
@@ -80,8 +80,9 @@
 
     build(0, 0)
     copies = []
+    send_at = bonds // chunk * 2 // 3 * chunk
     for begin in range(0, bonds, chunk):
-        if begin == chunk:
+        if begin == send_at:
             pl.semaphore_wait(barrier, n_time - 1)
             for ahead in range(1, n_time):
                 copies.append(

time: 68.5 us -> 69.3 us (1.012)
  Pallas kernels: 61.2 us -> 62.1 us
    pallas_call x1, Pallas kernels: 11.5 us -> 12.3 us  [per_device(): pl.pallas_call(functools.partial(kinetic_kernel, n_tiles, tile_len, 0.5 /...]
where the time goes in v5:
time: 69.3 us; the launch traced here: 69 us
  Pallas kernels  62.1 us (90%)
  local copies, waits for them, and re-layouts  2.83 us (4%)
  waiting for transfers between devices  2.83 us (4%)
  other arithmetic  1.17 us (2%)
    pallas_call x1, Pallas kernels, per_device(): pl.pallas_call(functools.partial(green_kernel, n_tiles, tile_len, 1.5 / m...  49.7 us
    pallas_call x1, Pallas kernels, per_device(): pl.pallas_call(functools.partial(kinetic_kernel, n_tiles, tile_len, 0.5 /...  12.3 us
    ppermute x1, waiting for transfers between devices, per_device(): lax.ppermute(sent, 'spin', [(i, n_spin - 1 - i) for i in range(n_spin)])  2.83 us
    unnamed x8, local copies, waits for them, and re-layouts  2.83 us
  transfers between devices with their start and end apart: 1, of which 1 were waited for; matrix products, arithmetic and copies ran while one was open for 0% of the time, Pallas kernels for 0%

profile of v5, /device:TPU:0, one launch (start us, length us, event | category | flops | bytes accessed | tf_op | source)
XLA Modules:
  0.0 69.0 jit_solution(14064245401528793761)
XLA Ops:
  0.0 0.0 copy-start
  0.0 0.7 %copy-done = s32[3072,2]{0,1:T(2,128)S(1)} copy-done((s32[3072,2]{0,1:T(2,128)S(1)}, s32[3072,2]{0,1:T(2,128)}, u32[]{:S(2)}) %copy-start) | copy-done | bytes 24600
  0.7 0.0 copy-start.1
  0.7 0.7 %copy-done.1 = f32[3072]{0:T(1024)S(1)} copy-done((f32[3072]{0:T(1024)S(1)}, f32[3072]{0:T(1024)}, u32[]{:S(2)}) %copy-start.1) | copy-done | bytes 12312
  1.4 0.0 copy-start.2
  1.4 0.7 %copy-done.2 = s32[4,768]{1,0:T(4,128)S(1)} copy-done((s32[4,768]{1,0:T(4,128)S(1)}, s32[4,768]{1,0:T(4,128)}, u32[]{:S(2)}) %copy-start.2) | copy-done | bytes 12312
  2.2 0.0 copy-start.3
  2.2 0.7 copy-done.3
  2.8 12.3 %kinetic.1 = (bf16[3,1536,256]{2,1,0:T(8,128)(2,1)S(1)}, s32[16,768]{1,0:T(8,128)S(1)}) custom-call(s32[3,6]{1,0:T(4,128)S(1)} %bitcast.7, s32[2,3072]{1,0:T(2,128)S(1)} %bitcast.5, f32[1,3072]{1,0:T(1,128)S(1)} %bitcast.6, s32[4,768]{1,0:T(4,128)S(1)} %copy-done.2), custom_call_target="tpu_custom_call" | custom-call | flops 4831838208 | bytes 786432 | tf_op jit(solution)/shard_map/kinetic/pallas_call | solution.py:255
  15.2 49.7 %green.1 = (f32[768,384]{1,0:T(8,128)S(1)}, f32[768,384]{1,0:T(8,128)S(1)}) custom-call(s32[3,6]{1,0:T(4,128)S(1)} %bitcast.8, s32[16,768]{1,0:T(8,128)S(1)} %get-tuple-element.9.field, bf16[3,1536,256]{2,1,0:T(8,128)(2,1)S(1)} %get-tuple-element.10.k_parts), custom_call_target="tpu_custom_call" | custom-call | flops 36238786560 | bytes 4718592 | tf_op jit(solution)/shard_map/green/pallas_call | solution.py:282
  64.9 0.1 collective-permute-start
  65.0 2.8 %collective-permute-done = f32[768,384]{1,0:T(8,128)S(1)} collective-permute-done((f32[768,384]{1,0:T(8,128)S(1)}, f32[768,384]{1,0:T(8,128)S(1)}, u32[]{:S(2)}, u32[]{:S(2)}) %collective-permute-start) | collective-permute-done | bytes 1179680 | tf_op jit(solution)/shard_map/ppermute | solution.py:306
  67.8 1.2 %multiply_bitcast_fusion = f32[1,1,768,384]{3,2,1,0:T(8,128)} fusion(f32[768,384]{1,0:T(8,128)S(1)} %get-tuple-element.11, f32[768,384]{1,0:T(8,128)S(1)} %collective-permute-done), kind=kLoop, calls=%fused_computation | loop fusion | flops 294912 | bytes 3538944 | tf_op jit(solution)/shard_map/broadcast_in_dim | solution.py:308
Async XLA Ops:
  0.0 0.7 %copy-start = (s32[3072,2]{0,1:T(2,128)S(1)}, s32[3072,2]{0,1:T(2,128)}, u32[]{:S(2)}) copy-start(s32[3072,2]{0,1:T(2,128)} %param.5) | copy-start | bytes 73732
  0.7 0.7 %copy-start.1 = (f32[3072]{0:T(1024)S(1)}, f32[3072]{0:T(1024)}, u32[]{:S(2)}) copy-start(f32[3072]{0:T(1024)} %param.6) | copy-start | bytes 36868
  1.4 0.7 %copy-start.2 = (s32[4,768]{1,0:T(4,128)S(1)}, s32[4,768]{1,0:T(4,128)}, u32[]{:S(2)}) copy-start(s32[4,768]{1,0:T(4,128)} %field.1) | copy-start | bytes 36868
  2.2 0.7 copy-start.3
  64.9 2.9 %collective-permute-start = (f32[768,384]{1,0:T(8,128)S(1)}, f32[768,384]{1,0:T(8,128)S(1)}, u32[]{:S(2)}, u32[]{:S(2)}) collective-permute-start(f32[768,384]{1,0:T(8,128)S(1)} %get-tuple-element.12), channel_id=1, source_target_pairs={{0,2},{2,0},{1,3},{3,1},{4,6},{6,4},{5,7},{7,5},{8,10},{10,8},{9,1... | collective-permute-start | bytes 3538952 | tf_op jit(solution)/shard_map/ppermute | solution.py:306
